TPU v7x, 32 devices: a whole 2x2x4 slice. The times are simulated.
32 devices in a mesh: seq: 2 (over x), tp: 16 (over z, y, core).
Axes of the slice: x: 2, y: 2, z: 4, core: 2. Of those that a mesh axis runs over, the one named last changes fastest.
Arguments:
- text_states: bfloat16 [8192, 768], P(('seq', 'tp')), may hold values from -6 to 6
- visual_maps: bfloat16 [1024, 256], P(('seq', 'tp'))
- text_boxes: int32 [2, 8192], P(None, ('seq', 'tp')), may hold values from 0 to 999
- text_lengths: int32 [16], replicated, may hold values from 64 to 512, as said below
- qkv_weight: bfloat16 [2, 3, 768, 768], replicated, may hold values from -0.21875 to 0.21875
- out_weight: bfloat16 [2, 768, 768], replicated, may hold values from -2.5 to 2.5
- attn_bias: float32 [2, 3, 768], replicated, may hold values from -3 to 3
- ffn_in: bfloat16 [2, 3072, 768], P(None, 'tp'), may hold values from -0.21875 to 0.21875
- ffn_in_bias: bfloat16 [2, 3072], P(None, 'tp'), may hold values from -3 to 3
- ffn_out: bfloat16 [2, 3072, 768], P(None, 'tp'), may hold values from -0.109375 to 0.109375
- ffn_out_bias: float32 [2, 768], replicated, may hold values from -3 to 3
- norm_gain: float32 [2, 2, 768], replicated, may hold values from 0.25 to 1.75
- norm_shift: float32 [2, 2, 768], replicated, may hold values from -3 to 3
- bias_table: float32 [160, 12], replicated, may hold values from -3 to 3
- vis_weight: bfloat16 [256, 768], replicated, may hold values from -0.375 to 0.375
- vis_bias: float32 [768], replicated, may hold values from -3 to 3
- bn_gain: float32 [256], replicated, may hold values from 0.25 to 1.75
- bn_shift: float32 [256], replicated, may hold values from -3 to 3
- cotangent: bfloat16 [9216, 768], P(('seq', 'tp')), may hold values from -6 to 6
Outputs:
- out_states: bfloat16 [9216, 768], P(('seq', 'tp'))
- grad_text: float32 [8192, 768], P(('seq', 'tp'))
- grad_maps: float32 [1024, 256], P(('seq', 'tp'))
- grad_qkv: float32 [2, 3, 768, 768], P(None, None, 'tp')
- grad_out_weight: float32 [2, 768, 768], P(None, 'tp')
- grad_attn_bias: float32 [2, 3, 768], replicated
- grad_ffn_in: float32 [2, 3072, 768], P(None, 'tp')
- grad_ffn_in_bias: float32 [2, 3072], P(None, 'tp')
- grad_ffn_out: float32 [2, 3072, 768], P(None, 'tp')
- grad_ffn_out_bias: float32 [2, 768], replicated
- grad_norm_gain: float32 [2, 2, 768], replicated
- grad_norm_shift: float32 [2, 2, 768], replicated
- grad_bias_table: float32 [160, 12], replicated
- grad_vis_weight: float32 [256, 768], replicated
- grad_vis_bias: float32 [768], replicated
- grad_bn_gain: float32 [256], replicated
- grad_bn_shift: float32 [256], replicated
Inputs may be any that keep to these rules, and one draw needn't show every extreme that they name: `text_lengths`: some page has all 512 text slots used.
All inputs are finite; a program needn't handle non-finite values.
Results may differ from a plain program's by a relative error of at most 0.035.
Values may be sent and summed in bfloat16 or wider, within the bound.
No kernel may reach another device: no remote copies, remote signals or barrier semaphores. Data moves between devices by JAX's collectives and lax.ppermute only.
A program may use at most 256 MiB of HBM per device.

v0:
```python
import jax
import jax.numpy as jnp
from jax import lax
from jax.sharding import PartitionSpec as P

HEADS = 12
HEAD_DIM = 64
VIS_TOK = 49
VIS_SLOTS = 64
POS_BINS = 32
BOX_BINS = 64
LAYERS = 2
PAIR_PAGES = 1


box_step = 16
grid_pitch = 143
grid_width = 7
norm_epsilon = 1e-05
masked_score = -1000000000.0


def swapped(block, axis, distance):
    count = lax.axis_size(axis)
    route = []
    for low in range(count):
        high = low | 1 << distance
        if high != low and high < count:
            route += [(low, high), (high, low)]
    return lax.ppermute(block, axis, route)


def layer_norm(values, gain_row, shift_row):
    center = values - jnp.mean(values, axis=-1, keepdims=True)
    spread = jnp.mean(center * center, axis=-1, keepdims=True)
    return center * lax.rsqrt(spread + norm_epsilon) * gain_row + shift_row


def gelu_exact(values):
    return jax.nn.gelu(values, approximate=False)


def half_meta(boxes_half, length, half_index):
    text_count = boxes_half.shape[-1]
    slot_count = VIS_SLOTS // 2
    text_place = half_index * text_count + jnp.arange(text_count, dtype=jnp.int32)
    slot_place = half_index * slot_count + jnp.arange(slot_count, dtype=jnp.int32)
    places = jnp.concatenate([text_place, slot_place])
    grid_x = slot_place % grid_width * grid_pitch + 71
    grid_y = slot_place // grid_width * grid_pitch + 71
    coord_x = jnp.concatenate([boxes_half[0], grid_x])
    coord_y = jnp.concatenate([boxes_half[1], grid_y])
    usable = jnp.concatenate([text_place < length, slot_place < VIS_TOK])
    return (places, coord_x, coord_y, usable)


def bucket_codes(query_meta, key_meta):
    pos_half = POS_BINS // 2
    box_half = BOX_BINS // 2
    near_code = (
        jnp.clip(key_meta[0][None, :] - query_meta[0][:, None], -pos_half, pos_half - 1) + pos_half
    )
    across = (
        jnp.clip(
            (key_meta[1][None, :] - query_meta[1][:, None]) // box_step, -box_half, box_half - 1
        )
        + box_half
        + POS_BINS
    )
    down_code = (
        jnp.clip(
            (key_meta[2][None, :] - query_meta[2][:, None]) // box_step, -box_half, box_half - 1
        )
        + box_half
        + POS_BINS
        + BOX_BINS
    )
    return (near_code, across, down_code)


def page_onehot(query_meta, key_meta):
    near_code, across, down_code = bucket_codes(query_meta, key_meta)
    bucket_ids = jnp.arange(POS_BINS + 2 * BOX_BINS, dtype=jnp.int32)
    hit_table = (
        (near_code[..., None] == bucket_ids)
        | (across[..., None] == bucket_ids)
        | (down_code[..., None] == bucket_ids)
    )
    return hit_table.astype(jnp.bfloat16)


def heads_of(values):
    return values.reshape(values.shape[0], values.shape[1], HEADS, HEAD_DIM)


def attention_scores(query_states, all_keys, score_bias, key_usable, scale_factor):
    raw_scores = (
        jnp.einsum(
            "pqhd,pkhd->phqk",
            heads_of(query_states),
            heads_of(all_keys),
            preferred_element_type=jnp.float32,
        )
        * scale_factor
        + score_bias
    )
    return jnp.where(key_usable[:, None, None, :], raw_scores, masked_score)


def body(
    text_states,
    visual_maps,
    text_boxes,
    text_lengths,
    qkv_weight,
    out_weight,
    attn_bias,
    ffn_in,
    ffn_in_bias,
    ffn_out,
    ffn_out_bias,
    norm_gain,
    norm_shift,
    bias_table,
    vis_weight,
    vis_bias,
    bn_gain,
    bn_shift,
    cotangent,
):
    half_index = lax.axis_index("tp") % 2
    pair_index = (lax.axis_index("seq") * lax.axis_size("tp") + lax.axis_index("tp")) // 2
    text_half = text_states.shape[0] // PAIR_PAGES
    slot_half = visual_maps.shape[0] // PAIR_PAGES
    page_rows = text_half + slot_half
    local_rows = PAIR_PAGES * page_rows
    model_width = text_states.shape[1]
    scale_factor = HEAD_DIM ** (-0.5)
    count_cells = text_lengths.shape[0] * VIS_TOK
    maps_float = visual_maps.astype(jnp.float32)
    slot_place = half_index * slot_half + jnp.arange(slot_half, dtype=jnp.int32)
    slot_mask = jnp.tile(slot_place < VIS_TOK, PAIR_PAGES)[:, None]
    local_sum = jnp.sum(jnp.where(slot_mask, maps_float, 0.0), axis=0)
    local_square = jnp.sum(jnp.where(slot_mask, maps_float * maps_float, 0.0), axis=0)
    total_sum, total_square = lax.psum((local_sum, local_square), ("seq", "tp"))
    channel_mean = total_sum / count_cells
    inverse_std = lax.rsqrt(total_square / count_cells - channel_mean * channel_mean + norm_epsilon)
    centered_hat = jnp.where(slot_mask, (maps_float - channel_mean) * inverse_std, 0.0)
    normalized = jnp.where(slot_mask, centered_hat * bn_gain + bn_shift, 0.0)
    normal_low = normalized.astype(jnp.bfloat16)
    visual_tokens = jnp.dot(normal_low, vis_weight, preferred_element_type=jnp.float32) + vis_bias
    text_float = text_states.astype(jnp.float32).reshape(PAIR_PAGES, text_half, model_width)
    states = jnp.concatenate(
        [text_float, visual_tokens.reshape(PAIR_PAGES, slot_half, model_width)], axis=1
    )
    lengths_here = lax.dynamic_slice_in_dim(text_lengths, pair_index * PAIR_PAGES, PAIR_PAGES, 0)
    own_boxes = text_boxes.reshape(2, PAIR_PAGES, text_half)
    partner_boxes = swapped(text_boxes, "tp", 0).reshape(2, PAIR_PAGES, text_half)

    def metas_for(boxes_all, which_half):
        return jax.vmap(
            lambda boxes_page, length: half_meta(boxes_page, length, which_half), in_axes=(1, 0)
        )(boxes_all, lengths_here)

    own_meta = metas_for(own_boxes, half_index)
    other_meta = metas_for(partner_boxes, 1 - half_index)
    key_meta = tuple(
        (
            jnp.concatenate([front_part, back_part], axis=1)
            for front_part, back_part in zip(own_meta, other_meta)
        )
    )
    key_usable = key_meta[3]
    query_items = tuple((jnp.repeat(part_meta, 2, axis=0) for part_meta in own_meta))
    key_items = tuple((part_meta.reshape(2 * PAIR_PAGES, page_rows) for part_meta in key_meta))
    table_high = bias_table.astype(jnp.bfloat16)
    table_rest = (bias_table - table_high.astype(jnp.float32)).astype(jnp.bfloat16)

    def bias_block(block_item):
        hit_table = page_onehot(block_item[0:4], block_item[4:8])
        high_part = jnp.einsum(
            "qkb,bh->hqk", hit_table, table_high, preferred_element_type=jnp.float32
        )
        return high_part + jnp.einsum(
            "qkb,bh->hqk", hit_table, table_rest, preferred_element_type=jnp.float32
        )

    bias_parts = lax.map(bias_block, query_items + key_items)
    score_bias = (
        bias_parts.reshape(PAIR_PAGES, 2, HEADS, page_rows, page_rows)
        .transpose(0, 2, 3, 1, 4)
        .reshape(PAIR_PAGES, HEADS, page_rows, 2 * page_rows)
    )
    saved_layers = []
    for layer_index in range(LAYERS):
        rounded = states.astype(jnp.bfloat16)
        projected = jnp.einsum(
            "prd,tde->tpre", rounded, qkv_weight[layer_index], preferred_element_type=jnp.float32
        )
        query_states = (projected[0] + attn_bias[layer_index, 0]).astype(jnp.bfloat16)
        key_states = projected[1].astype(jnp.bfloat16)
        value_states = (projected[2] + attn_bias[layer_index, 1]).astype(jnp.bfloat16)
        partner_keys, partner_values = swapped((key_states, value_states), "tp", 0)
        all_keys = jnp.concatenate([key_states, partner_keys], axis=1)
        all_values = jnp.concatenate([value_states, partner_values], axis=1)
        scores = attention_scores(query_states, all_keys, score_bias, key_usable, scale_factor)
        top_score = jnp.max(scores, axis=-1, keepdims=True)
        raised = jnp.exp(scores - top_score)
        denominator = jnp.sum(raised, axis=-1, keepdims=True)
        soft_weights = (raised / denominator).astype(jnp.bfloat16)
        log_total = top_score + jnp.log(denominator)
        context = jnp.einsum(
            "phqk,pkhd->pqhd",
            soft_weights,
            heads_of(all_values),
            preferred_element_type=jnp.float32,
        )
        context = context.reshape(PAIR_PAGES, page_rows, model_width).astype(jnp.bfloat16)
        attended = (
            jnp.einsum(
                "prd,de->pre", context, out_weight[layer_index], preferred_element_type=jnp.float32
            )
            + attn_bias[layer_index, 2]
        )
        residual_one = states + attended
        normed = layer_norm(residual_one, norm_gain[layer_index, 0], norm_shift[layer_index, 0])
        normed_low = normed.astype(jnp.bfloat16).reshape(local_rows, model_width)
        gathered = lax.all_gather(normed_low, "tp", axis=0, tiled=True)
        hidden = (
            jnp.einsum(
                "rd,fd->rf", gathered, ffn_in[layer_index], preferred_element_type=jnp.float32
            )
            + ffn_in_bias[layer_index]
        )
        activated = gelu_exact(hidden).astype(jnp.bfloat16)
        out_shard = ffn_out[layer_index]
        branch = (
            lax.psum_scatter(
                jnp.dot(activated, out_shard, preferred_element_type=jnp.float32).astype(
                    jnp.bfloat16
                ),
                "tp",
                scatter_dimension=0,
                tiled=True,
            ).astype(jnp.float32)
            + ffn_out_bias[layer_index]
        )
        ffn_saved = (gathered, hidden, activated)
        residual_two = normed + branch.reshape(PAIR_PAGES, page_rows, model_width)
        states = layer_norm(residual_two, norm_gain[layer_index, 1], norm_shift[layer_index, 1])
        saved_layers.append(
            (
                rounded,
                query_states,
                all_keys,
                all_values,
                log_total,
                context,
                residual_one,
                normed_low,
                residual_two,
                ffn_saved,
            )
        )
    out_states = states.reshape(local_rows, model_width).astype(jnp.bfloat16)
    gradient = cotangent.astype(jnp.float32).reshape(PAIR_PAGES, page_rows, model_width)
    grad_qkv_list = [None] * LAYERS
    grad_outw_list = [None] * LAYERS
    grad_bias_list = [None] * LAYERS
    grad_win_list = [None] * LAYERS
    grad_wout_list = [None] * LAYERS
    grad_bin_list = [None] * LAYERS
    grad_bout_list = [None] * LAYERS
    grad_gain_list = [None] * LAYERS
    grad_shift_list = [None] * LAYERS
    score_grad_list = [None] * LAYERS
    for layer_index in reversed(range(LAYERS)):
        (
            rounded,
            query_states,
            all_keys,
            all_values,
            log_total,
            context,
            residual_one,
            normed_low,
            residual_two,
            ffn_saved,
        ) = saved_layers[layer_index]
        norm_pull_two = jax.vjp(
            layer_norm, residual_two, norm_gain[layer_index, 1], norm_shift[layer_index, 1]
        )[1]
        grad_sum_two, grad_gain_two, grad_shift_two = norm_pull_two(gradient)
        branch_grad = grad_sum_two.astype(jnp.bfloat16).reshape(local_rows, model_width)
        grad_bout_list[layer_index] = jnp.sum(branch_grad.astype(jnp.float32), axis=0)
        gathered, hidden, activated = ffn_saved
        grad_rows = lax.all_gather(branch_grad, "tp", axis=0, tiled=True)
        act_grad = jnp.einsum(
            "re,fe->rf", grad_rows, ffn_out[layer_index], preferred_element_type=jnp.float32
        )
        hidden_grad = jax.vjp(gelu_exact, hidden)[1](act_grad)[0].astype(jnp.bfloat16)
        wout_part = jnp.einsum(
            "rf,re->fe", activated, grad_rows, preferred_element_type=jnp.float32
        )
        win_part = jnp.einsum(
            "rf,rd->fd", hidden_grad, gathered, preferred_element_type=jnp.float32
        )
        bin_part = jnp.sum(hidden_grad.astype(jnp.float32), axis=0)
        in_shard = ffn_in[layer_index]
        normed_grad = lax.psum_scatter(
            jnp.dot(hidden_grad, in_shard, preferred_element_type=jnp.float32).astype(jnp.bfloat16),
            "tp",
            scatter_dimension=0,
            tiled=True,
        ).astype(jnp.float32)
        grad_win_list[layer_index] = win_part
        grad_wout_list[layer_index] = wout_part
        grad_bin_list[layer_index] = bin_part
        grad_one = grad_sum_two + normed_grad.reshape(PAIR_PAGES, page_rows, model_width)
        norm_pull_one = jax.vjp(
            layer_norm, residual_one, norm_gain[layer_index, 0], norm_shift[layer_index, 0]
        )[1]
        grad_res_one, grad_gain_one, grad_shift_one = norm_pull_one(grad_one)
        grad_gain_list[layer_index] = jnp.stack([grad_gain_one, grad_gain_two])
        grad_shift_list[layer_index] = jnp.stack([grad_shift_one, grad_shift_two])
        attended_grad = grad_res_one.astype(jnp.bfloat16)
        grad_bias_out = jnp.sum(attended_grad.astype(jnp.float32), axis=(0, 1))
        grad_outw_list[layer_index] = jnp.einsum(
            "prd,pre->de", context, attended_grad, preferred_element_type=jnp.float32
        )
        context_grad = jnp.einsum(
            "pre,de->prd",
            attended_grad,
            out_weight[layer_index],
            preferred_element_type=jnp.float32,
        ).astype(jnp.bfloat16)
        scores = attention_scores(query_states, all_keys, score_bias, key_usable, scale_factor)
        soft_full = jnp.exp(scores - log_total)
        soft_low = soft_full.astype(jnp.bfloat16)
        prob_grad = jnp.einsum(
            "pqhd,pkhd->phqk",
            heads_of(context_grad),
            heads_of(all_values),
            preferred_element_type=jnp.float32,
        )
        score_grad = (
            soft_full * (prob_grad - jnp.sum(soft_full * prob_grad, axis=-1, keepdims=True))
        ).astype(jnp.bfloat16)
        score_grad_list[layer_index] = score_grad
        query_grad = (
            jnp.einsum(
                "phqk,pkhd->pqhd",
                score_grad,
                heads_of(all_keys),
                preferred_element_type=jnp.float32,
            )
            * scale_factor
        )
        key_grad_all = (
            jnp.einsum(
                "phqk,pqhd->pkhd",
                score_grad,
                heads_of(query_states),
                preferred_element_type=jnp.float32,
            )
            * scale_factor
        )
        value_grad_all = jnp.einsum(
            "phqk,pqhd->pkhd", soft_low, heads_of(context_grad), preferred_element_type=jnp.float32
        )
        key_grad_all = key_grad_all.reshape(PAIR_PAGES, 2 * page_rows, model_width)
        value_grad_all = value_grad_all.reshape(PAIR_PAGES, 2 * page_rows, model_width)
        back_keys, back_values = (
            swapped(key_grad_all[:, page_rows:].astype(jnp.bfloat16), "tp", 0).astype(jnp.float32),
            swapped(value_grad_all[:, page_rows:].astype(jnp.bfloat16), "tp", 0).astype(
                jnp.float32
            ),
        )
        query_low = query_grad.reshape(PAIR_PAGES, page_rows, model_width).astype(jnp.bfloat16)
        key_low = (key_grad_all[:, :page_rows] + back_keys).astype(jnp.bfloat16)
        value_low = (value_grad_all[:, :page_rows] + back_values).astype(jnp.bfloat16)
        stacked = jnp.stack([query_low, key_low, value_low])
        grad_qkv_list[layer_index] = jnp.einsum(
            "prd,tpre->tde", rounded, stacked, preferred_element_type=jnp.float32
        )
        grad_query_bias = jnp.sum(query_low.astype(jnp.float32), axis=(0, 1))
        grad_value_bias = jnp.sum(value_low.astype(jnp.float32), axis=(0, 1))
        grad_bias_list[layer_index] = jnp.stack([grad_query_bias, grad_value_bias, grad_bias_out])
        gradient = grad_res_one + jnp.einsum(
            "tpre,tde->prd", stacked, qkv_weight[layer_index], preferred_element_type=jnp.float32
        )
    score_stack = jnp.stack(score_grad_list).reshape(
        LAYERS, PAIR_PAGES, HEADS, page_rows, 2, page_rows
    )
    score_split = score_stack.transpose(1, 4, 0, 2, 3, 5).reshape(
        2 * PAIR_PAGES, LAYERS, HEADS, page_rows, page_rows
    )

    def table_block(block_item):
        hit_table = page_onehot(block_item[0:4], block_item[4:8])
        return jnp.einsum(
            "lhqk,qkb->bh", block_item[8], hit_table, preferred_element_type=jnp.float32
        )

    table_grad = jnp.sum(lax.map(table_block, query_items + key_items + (score_split,)), axis=0)
    grad_text = gradient[:, :text_half].reshape(PAIR_PAGES * text_half, model_width)
    token_grad = (
        gradient[:, text_half:].reshape(PAIR_PAGES * slot_half, model_width).astype(jnp.bfloat16)
    )
    vis_bias_grad = jnp.sum(token_grad.astype(jnp.float32), axis=0)
    vis_weight_grad = jnp.einsum(
        "rc,rd->cd", normal_low, token_grad, preferred_element_type=jnp.float32
    )
    normal_grad = jnp.where(
        slot_mask,
        jnp.einsum("rd,cd->rc", token_grad, vis_weight, preferred_element_type=jnp.float32),
        0.0,
    )
    part_gain = jnp.sum(normal_grad * centered_hat, axis=0)
    part_shift = jnp.sum(normal_grad, axis=0)
    bn_gain_grad, bn_shift_grad = lax.psum((part_gain, part_shift), ("seq", "tp"))
    hat_grad = normal_grad * bn_gain
    grad_maps = jnp.where(
        slot_mask,
        inverse_std
        * (
            hat_grad
            - bn_gain * bn_shift_grad / count_cells
            - centered_hat * (bn_gain * bn_gain_grad / count_cells)
        ),
        0.0,
    )
    qkv_shard, outw_shard = (
        lax.psum_scatter(
            jnp.stack(grad_qkv_list).astype(jnp.bfloat16), "tp", scatter_dimension=2, tiled=True
        ).astype(jnp.float32),
        lax.psum_scatter(
            jnp.stack(grad_outw_list)[:, None].astype(jnp.bfloat16),
            "tp",
            scatter_dimension=2,
            tiled=True,
        ).astype(jnp.float32),
    )
    qkv_total, outw_total, win_total, wout_total, bin_total = (
        lax.psum(qkv_shard.astype(jnp.bfloat16), "seq").astype(jnp.float32),
        lax.psum(outw_shard[:, 0].astype(jnp.bfloat16), "seq").astype(jnp.float32),
        lax.psum(jnp.stack(grad_win_list).astype(jnp.bfloat16), "seq").astype(jnp.float32),
        lax.psum(jnp.stack(grad_wout_list).astype(jnp.bfloat16), "seq").astype(jnp.float32),
        lax.psum(jnp.stack(grad_bin_list).astype(jnp.bfloat16), "seq").astype(jnp.float32),
    )
    bias_total, bout_total, gain_total, shift_total, table_total, visw_total, visb_total = lax.psum(
        (
            jnp.stack(grad_bias_list),
            jnp.stack(grad_bout_list),
            jnp.stack(grad_gain_list),
            jnp.stack(grad_shift_list),
            table_grad,
            vis_weight_grad,
            vis_bias_grad,
        ),
        ("seq", "tp"),
    )
    return (
        out_states,
        grad_text,
        grad_maps,
        qkv_total,
        outw_total,
        bias_total,
        win_total,
        bin_total,
        wout_total,
        bout_total,
        gain_total,
        shift_total,
        table_total,
        visw_total,
        visb_total,
        bn_gain_grad,
        bn_shift_grad,
    )


def solution(mesh):
    return jax.shard_map(
        body,
        mesh=mesh,
        in_specs=(
            P(("seq", "tp"), None),
            P(("seq", "tp"), None),
            P(None, ("seq", "tp")),
            P(),
            P(),
            P(),
            P(),
            P(None, "tp", None),
            P(None, "tp"),
            P(None, "tp", None),
            P(),
            P(),
            P(),
            P(),
            P(),
            P(),
            P(),
            P(),
            P(("seq", "tp"), None),
        ),
        out_specs=(
            P(("seq", "tp"), None),
            P(("seq", "tp"), None),
            P(("seq", "tp"), None),
            P(None, None, "tp", None),
            P(None, "tp", None),
            P(),
            P(None, "tp", None),
            P(None, "tp"),
            P(None, "tp", None),
            P(),
            P(),
            P(),
            P(),
            P(),
            P(),
            P(),
            P(),
        ),
        check_vma=False,
    )
```

profile of v0, /device:TPU:0, one launch (start us, length us, event | category | flops | bytes accessed | tf_op | source)
XLA Modules:
  0.0 1486.3 jit_solution(2664167390465264346)
XLA Ops:
  10.5 41.6 %all-reduce.2 = (f32[256]{0:T(256)S(1)}, f32[256]{0:T(256)S(1)}) all-reduce(f32[256]{0:T(256)S(1)} %get-tuple-element.536, f32[256]{0:T(256)S(1)} %get-tuple-element.535), channel_id=1, replica_groups=mesh['seq'=2,'tp'=16] {'seq','tp'}, use_global_device_ids=true, to_apply=%region_3.4 | all-reduce | flops 512 | bytes 4096 | tf_op jit(solution)/shard_map/psum | solution.py:145
  53.7 3.5 fusion.99
  76.1 91.4 %while.30 = (s32[]{:T(128)}, f32[2,12,288,288]{3,1,2,0:T(8,128)}, s32[2,288]{1,0:T(2,128)S(1)}, s32[2,288]{1,0:T(2,128)S(1)}, s32[2,288]{1,0:T(2,128)S(1)}, /*in...) while((s32[]{:T(128)}, f32[2,12,288,288]{3,1,2,0:T(8,128)}, ...), condition=%wide.region_5.6_spmd, body=%wide.region_4.5_spmd.sunk | while | flops 773950464 | bytes 95805696 | solution.py:188
  77.2 19.8 %fusion.324 = f32[288,288,12]{1,2,0:T(8,128)S(1)} fusion(s32[288,288]{1,0:T(8,128)S(1)} %fusion.320, s32[288,288]{1,0:T(8,128)S(1)} %fusion.322, s32[288,288]{1,0:T(8,128)S(1)} %clamp_add_fusion.4, bf16[160,12]{0,1:T(8,128)(2,1)S(1)} %get-tuple-element.863), kind=kOutput, calls=%fused_computation.5.clone.1 | convolution fusion | flops 384860160 | bytes 4980480 | tf_op jit(solution)/shard_map/while/body/eval_jaxpr/qkb,bh->hqk/dot_general | solution.py:184
  97.0 19.8 %bitcast_dynamic-update-slice_fusion.2 = f32[2,12,288,288]{3,1,2,0:T(8,128)S(1)} fusion(f32[2,12,288,288]{3,1,2,0:T(8,128)S(1)} %bitcast.331, s32[]{:T(128)S(6)} %copy.146, f32[288,288,12]{1,2,0:T(8,128)S(1)} %fusion.324, s32[288,288]{1,0:T(8,128)S(1)} %fusion.320, s32[288,288]{1,0:T(8,128)S(1)} %fusion.322, s32[288,288]{1,0:T(8,128)S(1)} %clamp_add_fusion.4, ...), kind=kOutput, calls=%fused_computation.7.clone.1 | convolution fusion | flops 385855488 | bytes 15491076 | tf_op jit(solution)/shard_map/while/body/eval_jaxpr/qkb,bh->hqk/dot_general | solution.py:181
  116.9 5.0 copy-done.5
  122.9 19.8 %fusion.324 = f32[288,288,12]{1,2,0:T(8,128)S(1)} fusion(s32[288,288]{1,0:T(8,128)S(1)} %fusion.320, s32[288,288]{1,0:T(8,128)S(1)} %fusion.322, s32[288,288]{1,0:T(8,128)S(1)} %clamp_add_fusion.4, bf16[160,12]{0,1:T(8,128)(2,1)S(1)} %get-tuple-element.863), kind=kOutput, calls=%fused_computation.5.clone.1 | convolution fusion | flops 384860160 | bytes 4980480 | tf_op jit(solution)/shard_map/while/body/eval_jaxpr/qkb,bh->hqk/dot_general | solution.py:184
  142.7 19.8 %bitcast_dynamic-update-slice_fusion.2 = f32[2,12,288,288]{3,1,2,0:T(8,128)S(1)} fusion(f32[2,12,288,288]{3,1,2,0:T(8,128)S(1)} %bitcast.331, s32[]{:T(128)S(6)} %copy.146, f32[288,288,12]{1,2,0:T(8,128)S(1)} %fusion.324, s32[288,288]{1,0:T(8,128)S(1)} %fusion.320, s32[288,288]{1,0:T(8,128)S(1)} %fusion.322, s32[288,288]{1,0:T(8,128)S(1)} %clamp_add_fusion.4, ...), kind=kOutput, calls=%fused_computation.7.clone.1 | convolution fusion | flops 385855488 | bytes 15491076 | tf_op jit(solution)/shard_map/while/body/eval_jaxpr/qkb,bh->hqk/dot_general | solution.py:181
  162.6 5.0 copy-done.5
  168.2 16.5 %copy.105 = f32[1,12,288,2,288]{4,3,2,1,0:T(2,128)} copy(f32[1,12,288,2,288]{4,1,2,3,0:T(8,128)} %bitcast.332) | data formatting | bytes 15925248 | tf_op jit(solution)/shard_map/transpose | solution.py:191
  184.7 13.1 reshape.1573
  199.2 5.3 fusion.256
  209.2 5.0 fusion.116
  216.5 66.5 %all-gather.5.cloned.1.call-done = bf16[4608,768]{1,0:T(8,128)(2,1)} async-done(((bf16[288,768]{1,0:T(8,128)(2,1)}), bf16[4608,768]{1,0:T(8,128)(2,1)}) %all-gather.5.cloned.1.call-update) | async-done | bytes 7077904 | tf_op jit(solution)/shard_map/all_gather | solution.py:228
  283.0 12.8 multiply_convert_fusion.3
  297.1 5.0 convolution_convert_fusion.3
  303.5 87.3 %reduce-scatter.6.cloned.1.call-done = bf16[288,768]{1,0:T(8,128)(2,1)} async-done(((bf16[4608,768]{1,0:T(8,128)(2,1)}), bf16[288,768]{1,0:T(8,128)(2,1)}) %reduce-scatter.6.cloned.1.call-update) | async-done | bytes 442384 | tf_op jit(solution)/shard_map/reduce_scatter | solution.py:238
  392.6 3.3 fusion.102
  411.0 6.5 fusion.258
  422.2 5.0 fusion.115
  429.6 66.1 %all-gather.7.cloned.1.call-done = bf16[4608,768]{1,0:T(8,128)(2,1)} async-done(((bf16[288,768]{1,0:T(8,128)(2,1)}), bf16[4608,768]{1,0:T(8,128)(2,1)}) %all-gather.7.cloned.1.call-update) | async-done | bytes 7077904 | tf_op jit(solution)/shard_map/all_gather | solution.py:228
  495.6 12.8 multiply_convert_fusion.2
  509.7 5.0 convolution_convert_fusion.2
  514.8 88.7 %reduce-scatter.8.cloned.1.call-done = bf16[288,768]{1,0:T(8,128)(2,1)} async-done(((bf16[4608,768]{1,0:T(8,128)(2,1)}), bf16[288,768]{1,0:T(8,128)(2,1)}) %reduce-scatter.8.cloned.1.call-update) | async-done | bytes 442384 | tf_op jit(solution)/shard_map/reduce_scatter | solution.py:238
  609.8 66.0 %all-gather.9.cloned.1.call-done = bf16[4608,768]{1,0:T(8,128)(2,1)} async-done(((bf16[288,768]{1,0:T(8,128)(2,1)}), bf16[4608,768]{1,0:T(8,128)(2,1)}) %all-gather.9.cloned.1.call-update) | async-done | bytes 7077904 | tf_op jit(solution)/shard_map/all_gather | solution.py:297
  675.8 8.6 fusion.260
  685.6 4.9 convolution_convert_fusion.1
  693.5 85.7 %reduce-scatter.10.cloned.1.call-done = bf16[288,768]{1,0:T(8,128)(2,1)} async-done(((bf16[4608,768]{1,0:T(8,128)(2,1)}), bf16[288,768]{1,0:T(8,128)(2,1)}) %reduce-scatter.10.cloned.1.call-update) | async-done | bytes 442384 | tf_op jit(solution)/shard_map/reduce_scatter | solution.py:310
  787.1 5.3 fusion.69
  795.6 7.1 multiply_reduce_fusion.1
  813.7 4.7 convert_reduce_fusion.2
  823.9 4.2 multiply_reduce_fusion.3
  829.5 66.3 %all-gather.11.cloned.1.call-done = bf16[4608,768]{1,0:T(8,128)(2,1)} async-done(((bf16[288,768]{1,0:T(8,128)(2,1)}), bf16[4608,768]{1,0:T(8,128)(2,1)}) %all-gather.11.cloned.1.call-update) | async-done | bytes 7077904 | tf_op jit(solution)/shard_map/all_gather | solution.py:297
  895.7 8.6 fusion.261
  905.6 4.9 convolution_convert_fusion
  916.4 5.7 convert_bitcast_fusion
  922.1 77.2 %reduce-scatter.12.cloned.1.call-done = bf16[288,768]{1,0:T(8,128)(2,1)} async-done(((bf16[4608,768]{1,0:T(8,128)(2,1)}), bf16[288,768]{1,0:T(8,128)(2,1)}) %reduce-scatter.12.cloned.1.call-update) | async-done | bytes 442384 | tf_op jit(solution)/shard_map/reduce_scatter | solution.py:310
  1005.6 4.8 fusion.67
  1013.6 6.7 multiply_reduce_fusion
  1030.0 4.5 convert_reduce_fusion.3
  1043.3 3.5 pad_maximum_fusion
  1046.8 18.3 %copy.127 = bf16[2,3,768,768]{3,0,1,2:T(2,128)(2,1)} copy(bf16[2,3,768,768]{2,3,1,0:T(8,128)(2,1)} %pad_maximum_fusion) | data formatting | bytes 14155776 | tf_op jit(solution)/shard_map/stack | solution.py:435
  1066.5 5.4 fusion.135
  1071.9 5.3 fusion.133
  1077.2 11.7 stack.236
  1089.1 5.9 copy.129
  1099.4 4.9 psum.120
  1104.9 4.8 fusion.132
  1110.7 4.7 fusion.134
  1116.2 11.7 stack.235
  1128.0 5.7 copy.128
  1136.4 9.8 maximum_bitcast_fusion
  1146.4 64.5 %while.31 = (s32[]{:T(128)}, f32[2,160,12]{1,2,0:T(8,128)}, s32[2,288]{1,0:T(2,128)S(1)}, s32[2,288]{1,0:T(2,128)S(1)}, s32[2,288]{1,0:T(2,128)S(1)}, /*index=5*...) while((s32[]{:T(128)}, f32[2,160,12]{1,2,0:T(8,128)}, ...), condition=%wide.region_67.68_spmd, body=%wide.region_65.67_spmd.sunk | while | flops 391080960 | bytes 15741313 | solution.py:405
  1149.0 3.4 convert_reduce_fusion.12
  1152.4 5.1 copy.141
  1157.5 21.1 %fusion.332 = f32[2,160,12]{1,2,0:T(8,128)} fusion(f32[2,160,12]{1,2,0:T(8,128)} %get-tuple-element.876, s32[]{:T(128)S(6)} %copy.152, bf16[12,288,288]{1,0,2:T(8,128)(2,1)} %copy.141, s32[288,288]{0,1:T(8,128)} %fusion.328, s32[288,288]{0,1:T(8,128)} %fusion.330, s32[288,288]{0,1:T(8,128)S(1)} %clamp_add_fusion.5), kind=kOutput, calls=%fused_computation.62.clone.1 | convolution fusion | flops 384860160 | bytes 4771844 | tf_op jit(solution)/shard_map/while/body/eval_jaxpr/lhqk,qkb->bh/dot_general | solution.py:401
  1181.2 3.5 convert_reduce_fusion.12
  1184.7 5.1 copy.141
  1189.8 21.1 %fusion.332 = f32[2,160,12]{1,2,0:T(8,128)} fusion(f32[2,160,12]{1,2,0:T(8,128)} %get-tuple-element.876, s32[]{:T(128)S(6)} %copy.152, bf16[12,288,288]{1,0,2:T(8,128)(2,1)} %copy.141, s32[288,288]{0,1:T(8,128)} %fusion.328, s32[288,288]{0,1:T(8,128)} %fusion.330, s32[288,288]{0,1:T(8,128)S(1)} %clamp_add_fusion.5), kind=kOutput, calls=%fused_computation.62.clone.1 | convolution fusion | flops 384860160 | bytes 4771844 | tf_op jit(solution)/shard_map/while/body/eval_jaxpr/lhqk,qkb->bh/dot_general | solution.py:401
  1217.2 64.6 %reduce-scatter.14.cloned.1.call-done = bf16[2,1,48,768]{3,2,1,0:T(8,128)(2,1)} async-done(((bf16[2,1,768,768]{3,2,1,0:T(8,128)(2,1)}), bf16[2,1,48,768]{3,2,1,0:T(8,128)(2,1)}) %reduce-scatter.14.cloned.1.call-update) | async-done | bytes 147472 | tf_op jit(solution)/shard_map/reduce_scatter | solution.py:437
  1284.1 3.9 fusion.125
  1288.3 42.5 %all-reduce.1 = (f32[256]{0:T(256)S(1)}, f32[256]{0:T(256)S(1)}, f32[2,3,768]{2,1,0:T(4,128)S(1)}, f32[2,768]{1,0:T(2,128)}, f32[2,2,768]{2,1,0:T(2,128)}, /*ind...) all-reduce(f32[256]{0:T(256)S(1)} %get-tuple-element.528, ...), channel_id=1, replica_groups=mesh['seq'=2,'tp'=16] {'seq','tp'}, use_global_device_ids=true, to_apply=%region_35.36 | all-reduce | flops 15488 | bytes 123904 | tf_op jit(solution)/shard_map/psum | solution.py:421
  1334.4 7.9 all-reduce.12.cloned.1.call-done
  1349.2 127.7 %all-reduce.8.cloned.1.call-done = f32[256,768]{1,0:T(8,128)} async-done(((f32[256,768]{1,0:T(8,128)}), f32[256,768]{1,0:T(8,128)}) %all-reduce.8.cloned.1.call-update) | async-done | bytes 786448 | tf_op jit(solution)/shard_map/psum | solution.py:451
  (630 shorter events, 172.9 us)
Async XLA Ops:
  7.2 45.5 %copy-start = (bf16[256,768]{1,0:T(8,128)(2,1)S(1)}, bf16[256,768]{1,0:T(8,128)(2,1)}, u32[]{:S(2)}) copy-start(bf16[256,768]{1,0:T(8,128)(2,1)} %param.37) | copy-start | bytes 1179652
  7.2 275.8 %all-gather.5.cloned.1.call-start = ((), (), s32[]{:S(2)}) async-start(), calls=%async_computation.5 | async-start | bytes 7520256 | tf_op jit(solution)/shard_map/all_gather | solution.py:228
  7.2 67.8 %collective-permute-start.2 = (s32[2,256]{1,0:T(2,128)}, s32[2,256]{1,0:T(2,128)}, u32[]{:S(2)}, u32[]{:S(2)}) collective-permute-start(s32[2,256]{1,0:T(2,128)} %param.25), channel_id=1, source_target_pairs={{0,1},{1,0},{2,3},{3,2},{4,5},{5,4},{6,7},{7,6},{8,9},{9,8},{10,11... | collective-permute-start | bytes 6152 | tf_op jit(solution)/shard_map/ppermute | solution.py:30
  7.8 44.4 %copy-start.132 = (pred[32]{0:T(512)(128)(4,1)}, pred[32]{0:T(512)(128)(4,1)S(1)}, u32[]{:S(2)}) copy-start(pred[32]{0:T(512)(128)(4,1)S(1)} %broadcast_compare_fusion) | copy-start | bytes 100
  58.0 139.7 %collective-permute-start.1 = (bf16[1,288,768]{2,1,0:T(8,128)(2,1)}, bf16[1,288,768]{2,1,0:T(8,128)(2,1)}, u32[]{:S(2)}, u32[]{:S(2)}) collective-permute-start(bf16[1,288,768]{2,1,0:T(8,128)(2,1)} %slice_bitcast_fusion.1), channel_id=1, source_target_pairs={{0,1},{1,0},{2,3},{3,2},{4,5},{5,4},{6,7},{7,6},{8,9},{9,8},{10,11... | collective-permute-start | bytes 1327112 | tf_op jit(solution)/shard_map/ppermute | solution.py:30
  59.5 148.3 %collective-permute-start = (bf16[1,288,768]{2,1,0:T(8,128)(2,1)}, bf16[1,288,768]{2,1,0:T(8,128)(2,1)}, u32[]{:S(2)}, u32[]{:S(2)}) collective-permute-start(bf16[1,288,768]{2,1,0:T(8,128)(2,1)} %fusion.157), channel_id=1, source_target_pairs={{0,1},{1,0},{2,3},{3,2},{4,5},{5,4},{6,7},{7,6},{8,9},{9,8},{10,11... | collective-permute-start | bytes 1327112 | tf_op jit(solution)/shard_map/ppermute | solution.py:30
  76.2 20.8 %slice-start.6 = ((s8[14155776]{0:T(1024)(128)(4,1)}), s8[4194304]{0:T(1024)(128)(4,1)S(1)}, s32[]{:S(2)}) async-start(s8[14155776]{0:T(1024)(128)(4,1)} %bitcast.330), calls=%async_computation.23 | async-start | bytes 8388608 | tf_op jit(solution)/shard_map/while
  77.2 19.8 %slice-start.7 = ((s8[14155776]{0:T(1024)(128)(4,1)}), s8[4194304]{0:T(1024)(128)(4,1)S(1)}, s32[]{:S(2)}) async-start(s8[14155776]{0:T(1024)(128)(4,1)} %bitcast.330), calls=%async_computation.24 | async-start | bytes 8388608 | tf_op jit(solution)/shard_map/while
  77.2 19.8 %slice-start.8 = ((s8[14155776]{0:T(1024)(128)(4,1)}), s8[4194304]{0:T(1024)(128)(4,1)S(1)}, s32[]{:S(2)}) async-start(s8[14155776]{0:T(1024)(128)(4,1)} %bitcast.330), calls=%async_computation.25 | async-start | bytes 8388608 | tf_op jit(solution)/shard_map/while
  77.2 19.8 %slice-start.9 = ((s8[14155776]{0:T(1024)(128)(4,1)}), s8[1572864]{0:T(1024)(128)(4,1)S(1)}, s32[]{:S(2)}) async-start(s8[14155776]{0:T(1024)(128)(4,1)} %bitcast.330), calls=%async_computation.26 | async-start | bytes 3145728 | tf_op jit(solution)/shard_map/while
  121.9 20.8 %slice-start.6 = ((s8[14155776]{0:T(1024)(128)(4,1)}), s8[4194304]{0:T(1024)(128)(4,1)S(1)}, s32[]{:S(2)}) async-start(s8[14155776]{0:T(1024)(128)(4,1)} %bitcast.330), calls=%async_computation.23 | async-start | bytes 8388608 | tf_op jit(solution)/shard_map/while
  122.9 19.8 %slice-start.7 = ((s8[14155776]{0:T(1024)(128)(4,1)}), s8[4194304]{0:T(1024)(128)(4,1)S(1)}, s32[]{:S(2)}) async-start(s8[14155776]{0:T(1024)(128)(4,1)} %bitcast.330), calls=%async_computation.24 | async-start | bytes 8388608 | tf_op jit(solution)/shard_map/while
  122.9 19.8 %slice-start.8 = ((s8[14155776]{0:T(1024)(128)(4,1)}), s8[4194304]{0:T(1024)(128)(4,1)S(1)}, s32[]{:S(2)}) async-start(s8[14155776]{0:T(1024)(128)(4,1)} %bitcast.330), calls=%async_computation.25 | async-start | bytes 8388608 | tf_op jit(solution)/shard_map/while
  122.9 19.8 %slice-start.9 = ((s8[14155776]{0:T(1024)(128)(4,1)}), s8[1572864]{0:T(1024)(128)(4,1)S(1)}, s32[]{:S(2)}) async-start(s8[14155776]{0:T(1024)(128)(4,1)} %bitcast.330), calls=%async_computation.26 | async-start | bytes 3145728 | tf_op jit(solution)/shard_map/while
  167.6 17.1 %copy-start.65 = (s32[2,288]{1,0:T(2,128)}, s32[2,288]{1,0:T(2,128)S(1)}, u32[]{:S(2)}) copy-start(s32[2,288]{1,0:T(2,128)S(1)} %get-tuple-element.975) | copy-start | bytes 6916
  214.3 81.5 %copy-start.165 = (bf16[12,64,288]{2,1,0:T(8,128)(2,1)}, bf16[12,64,288]{2,1,0:T(8,128)(2,1)S(1)}, u32[]{:S(2)}) copy-start(bf16[12,64,288]{2,1,0:T(8,128)(2,1)S(1)} %fusion.116) | copy-start | bytes 1327108
  214.3 68.6 %copy-start.43 = (bf16[2,192,768]{2,1,0:T(8,128)(2,1)S(1)}, bf16[2,192,768]{2,1,0:T(8,128)(2,1)}, u32[]{:S(2)}) copy-start(bf16[2,192,768]{2,1,0:T(8,128)(2,1)} %param.30) | copy-start | bytes 1769476
  215.1 175.8 %copy-start.89 = (f32[288]{0:T(512)}, f32[288]{0:T(512)S(1)}, u32[]{:S(2)}) copy-start(f32[288]{0:T(512)S(1)} %broadcast_multiply_fusion.3) | copy-start | bytes 3460
  215.3 80.4 %copy-start.110 = (f32[288]{0:T(512)}, f32[288]{0:T(512)S(1)}, u32[]{:S(2)}) copy-start(f32[288]{0:T(512)S(1)} %multiply_reduce_fusion.11) | copy-start | bytes 3460
  215.4 175.5 %copy-start.93 = (f32[288]{0:T(512)}, f32[288]{0:T(512)S(1)}, u32[]{:S(2)}) copy-start(f32[288]{0:T(512)S(1)} %fusion.206) | copy-start | bytes 3460
  216.4 174.4 %reduce-scatter.6.cloned.1.call-start = ((), (), s32[]{:S(2)}) async-start(), calls=%async_computation.6 | async-start | bytes 7520256 | tf_op jit(solution)/shard_map/reduce_scatter | solution.py:238
  302.1 90.5 %copy-start.120 = (f32[768]{0:T(1024)S(1)}, f32[768]{0:T(1024)}, u32[]{:S(2)}) copy-start(f32[768]{0:T(1024)} %get-tuple-element.690) | copy-start | bytes 9220
  302.1 90.5 %copy-start.145 = (f32[768]{0:T(1024)S(1)}, f32[768]{0:T(1024)}, u32[]{:S(2)}) copy-start(f32[768]{0:T(1024)} %get-tuple-element.542) | copy-start | bytes 9220
  302.1 193.5 %all-gather.7.cloned.1.call-start = ((), (), s32[]{:S(2)}) async-start(), calls=%async_computation.7 | async-start | bytes 7520256 | tf_op jit(solution)/shard_map/all_gather | solution.py:228
  302.9 103.3 %copy-start.87 = (f32[12,64]{1,0:T(8,128)}, f32[12,64]{1,0:T(8,128)S(1)}, u32[]{:S(2)}) copy-start(f32[12,64]{1,0:T(8,128)S(1)} %add.861) | copy-start | bytes 9220
  392.2 35.0 %copy-start.12 = (f32[288,768]{1,0:T(8,128)}, f32[288,768]{1,0:T(8,128)S(1)}, u32[]{:S(2)}) copy-start(f32[288,768]{1,0:T(8,128)S(1)} %get-tuple-element.620) | copy-start | bytes 2654212
  392.3 35.0 %copy-start.117 = (f32[288]{0:T(512)}, f32[288]{0:T(512)S(1)}, u32[]{:S(2)}) copy-start(f32[288]{0:T(512)S(1)} %broadcast_multiply_fusion.2) | copy-start | bytes 3460
  392.5 34.8 %copy-start.141 = (f32[288]{0:T(512)}, f32[288]{0:T(512)S(1)}, u32[]{:S(2)}) copy-start(f32[288]{0:T(512)S(1)} %fusion.207) | copy-start | bytes 3460
  402.2 6.7 collective-permute-start.4
  404.1 16.7 %collective-permute-start.3 = (bf16[1,288,768]{2,1,0:T(8,128)(2,1)}, bf16[1,288,768]{2,1,0:T(8,128)(2,1)}, u32[]{:S(2)}, u32[]{:S(2)}) collective-permute-start(bf16[1,288,768]{2,1,0:T(8,128)(2,1)} %fusion.156), channel_id=1, source_target_pairs={{0,1},{1,0},{2,3},{3,2},{4,5},{5,4},{6,7},{7,6},{8,9},{9,8},{10,11... | collective-permute-start | bytes 1327112 | tf_op jit(solution)/shard_map/ppermute | solution.py:30
  428.0 175.5 %copy-start.91 = (f32[288]{0:T(512)}, f32[288]{0:T(512)S(1)}, u32[]{:S(2)}) copy-start(f32[288]{0:T(512)S(1)} %broadcast_multiply_fusion.1) | copy-start | bytes 3460
  428.3 80.1 %copy-start.114 = (f32[288]{0:T(512)}, f32[288]{0:T(512)S(1)}, u32[]{:S(2)}) copy-start(f32[288]{0:T(512)S(1)} %multiply_reduce_fusion.9) | copy-start | bytes 3460
  428.3 175.2 %copy-start.95 = (f32[288]{0:T(512)}, f32[288]{0:T(512)S(1)}, u32[]{:S(2)}) copy-start(f32[288]{0:T(512)S(1)} %fusion.208) | copy-start | bytes 3460
  429.4 174.1 %reduce-scatter.8.cloned.1.call-start = ((), (), s32[]{:S(2)}) async-start(), calls=%async_computation.8 | async-start | bytes 7520256 | tf_op jit(solution)/shard_map/reduce_scatter | solution.py:238
  514.7 88.8 %copy-start.122 = (f32[768]{0:T(1024)S(1)}, f32[768]{0:T(1024)}, u32[]{:S(2)}) copy-start(f32[768]{0:T(1024)} %get-tuple-element.545) | copy-start | bytes 9220
  514.7 90.4 %copy-start.38 = (bf16[288,768]{1,0:T(8,128)(2,1)S(1)}, bf16[288,768]{1,0:T(8,128)(2,1)}, u32[]{:S(2)}) copy-start(bf16[288,768]{1,0:T(8,128)(2,1)} %param.41) | copy-start | bytes 1327108
  514.7 90.5 %copy-start.98 = (f32[768]{0:T(1024)S(1)}, f32[768]{0:T(1024)}, u32[]{:S(2)}) copy-start(f32[768]{0:T(1024)} %get-tuple-element.691) | copy-start | bytes 9220
  514.8 161.0 %all-gather.9.cloned.1.call-start = ((), (), s32[]{:S(2)}) async-start(), calls=%async_computation.9 | async-start | bytes 7520256 | tf_op jit(solution)/shard_map/all_gather | solution.py:297
  609.5 169.7 %reduce-scatter.10.cloned.1.call-start = ((), (), s32[]{:S(2)}) async-start(), calls=%async_computation.10 | async-start | bytes 7520256 | tf_op jit(solution)/shard_map/reduce_scatter | solution.py:310
  690.5 88.7 %copy-start.92 = (f32[288]{0:T(512)S(1)}, f32[288]{0:T(512)}, u32[]{:S(2)}) copy-start(f32[288]{0:T(512)} %copy-done.91) | copy-start | bytes 3460
  690.5 88.7 %copy-start.96 = (f32[288]{0:T(512)S(1)}, f32[288]{0:T(512)}, u32[]{:S(2)}) copy-start(f32[288]{0:T(512)} %copy-done.95) | copy-start | bytes 3460
  690.6 90.9 %copy-start.115 = (f32[288]{0:T(512)S(1)}, f32[288]{0:T(512)}, u32[]{:S(2)}) copy-start(f32[288]{0:T(512)} %copy-done.114) | copy-start | bytes 3460
  690.6 205.1 %all-gather.11.cloned.1.call-start = ((), (), s32[]{:S(2)}) async-start(), calls=%async_computation.11 | async-start | bytes 7520256 | tf_op jit(solution)/shard_map/all_gather | solution.py:297
  795.6 26.6 %collective-permute-start.6 = (bf16[1,288,768]{2,1,0:T(8,128)(2,1)}, bf16[1,288,768]{2,1,0:T(8,128)(2,1)}, u32[]{:S(2)}, u32[]{:S(2)}) collective-permute-start(bf16[1,288,768]{2,1,0:T(8,128)(2,1)} %copy.135), channel_id=1, source_target_pairs={{0,1},{1,0},{2,3},{3,2},{4,5},{5,4},{6,7},{7,6},{8,9},{9,8},{10,11... | collective-permute-start | bytes 1327112 | tf_op jit(solution)/shard_map/ppermute | solution.py:30
  813.2 10.5 collective-permute-start.5
  829.4 169.9 %reduce-scatter.12.cloned.1.call-start = ((), (), s32[]{:S(2)}) async-start(), calls=%async_computation.12 | async-start | bytes 7520256 | tf_op jit(solution)/shard_map/reduce_scatter | solution.py:310
  910.6 304.5 %all-reduce.10.cloned.1.call-start = ((), (), s32[]{:S(2)}) async-start(), calls=%async_computation.15 | async-start | bytes 14155776
  916.3 82.9 %copy-start.90 = (f32[288]{0:T(512)S(1)}, f32[288]{0:T(512)}, u32[]{:S(2)}) copy-start(f32[288]{0:T(512)} %copy-done.89) | copy-start | bytes 3460
  916.3 82.9 %copy-start.94 = (f32[288]{0:T(512)S(1)}, f32[288]{0:T(512)}, u32[]{:S(2)}) copy-start(f32[288]{0:T(512)} %copy-done.93) | copy-start | bytes 3460
  916.3 85.2 %copy-start.111 = (f32[288]{0:T(512)S(1)}, f32[288]{0:T(512)}, u32[]{:S(2)}) copy-start(f32[288]{0:T(512)} %copy-done.110) | copy-start | bytes 3460
  1013.5 23.2 %collective-permute-start.8 = (bf16[1,288,768]{2,1,0:T(8,128)(2,1)}, bf16[1,288,768]{2,1,0:T(8,128)(2,1)}, u32[]{:S(2)}, u32[]{:S(2)}) collective-permute-start(bf16[1,288,768]{2,1,0:T(8,128)(2,1)} %copy.139), channel_id=1, source_target_pairs={{0,1},{1,0},{2,3},{3,2},{4,5},{5,4},{6,7},{7,6},{8,9},{9,8},{10,11... | collective-permute-start | bytes 1327112 | tf_op jit(solution)/shard_map/ppermute | solution.py:30
  1029.5 9.1 collective-permute-start.7
  1065.0 216.7 %reduce-scatter.14.cloned.1.call-start = ((), (), s32[]{:S(2)}) async-start(), calls=%async_computation.13 | async-start | bytes 2506752 | tf_op jit(solution)/shard_map/reduce_scatter | solution.py:437
  1136.1 206.2 %all-reduce.12.cloned.1.call-start = ((), (), s32[]{:S(2)}) async-start(), calls=%async_computation.16 | async-start | bytes 3538944 | tf_op jit(solution)/shard_map/psum | solution.py:445
  1146.3 65.3 %copy-start.126 = (f32[768]{0:T(1024)S(1)}, f32[768]{0:T(1024)}, u32[]{:S(2)}) copy-start(f32[768]{0:T(1024)} %get-tuple-element.521) | copy-start | bytes 9220
  1146.3 66.0 %copy-start.102 = (f32[12,64]{1,0:T(8,128)S(1)}, f32[12,64]{1,0:T(8,128)}, u32[]{:S(2)}) copy-start(f32[12,64]{1,0:T(8,128)} %get-tuple-element.674) | copy-start | bytes 9220
  1146.3 136.9 %copy-start.108 = (f32[1,2,768]{2,1,0:T(2,128)S(1)}, f32[1,2,768]{2,1,0:T(2,128)}, u32[]{:S(2)}) copy-start(f32[1,2,768]{2,1,0:T(2,128)} %maximum_bitcast_fusion.20) | copy-start | bytes 18436
  1146.3 136.9 %copy-start.109 = (f32[1,2,768]{2,1,0:T(2,128)S(1)}, f32[1,2,768]{2,1,0:T(2,128)}, u32[]{:S(2)}) copy-start(f32[1,2,768]{2,1,0:T(2,128)} %maximum_bitcast_fusion.22) | copy-start | bytes 18436
  1146.3 137.6 %copy-start.97 = (f32[1,3,768]{2,1,0:T(4,128)S(1)}, f32[1,3,768]{2,1,0:T(4,128)}, u32[]{:S(2)}) copy-start(f32[1,3,768]{2,1,0:T(4,128)} %maximum_bitcast_fusion.18) | copy-start | bytes 27652
  1281.8 195.1 %all-reduce.8.cloned.1.call-start = ((), (), s32[]{:S(2)}) async-start(), calls=%async_computation.14 | async-start | bytes 1572864 | tf_op jit(solution)/shard_map/psum | solution.py:451
  1284.1 47.4 %copy-start.119 = (f32[256]{0:T(256)S(1)}, f32[256]{0:T(256)}, u32[]{:S(2)}) copy-start(f32[256]{0:T(256)} %param.39) | copy-start | bytes 3076
  1284.1 47.4 %copy-start.144 = (f32[256]{0:T(256)S(1)}, f32[256]{0:T(256)}, u32[]{:S(2)}) copy-start(f32[256]{0:T(256)} %param.40) | copy-start | bytes 3076
  1330.9 18.4 %copy-start.157 = (f32[256]{0:T(256)}, f32[256]{0:T(256)S(1)}, u32[]{:S(2)}) copy-start(f32[256]{0:T(256)S(1)} %get-tuple-element.910) | copy-start | bytes 3076
  1330.9 18.4 %copy-start.158 = (f32[256]{0:T(256)}, f32[256]{0:T(256)S(1)}, u32[]{:S(2)}) copy-start(f32[256]{0:T(256)S(1)} %get-tuple-element.911) | copy-start | bytes 3076
  (144 other events, 764.0 us)
Sparse Core Ops, SparseCore 0:
  216.5 66.4 all-gather.4
  302.3 88.5 reduce-scatter.5
  429.5 66.1 all-gather.6
  514.9 88.5 reduce-scatter.7
  609.6 66.0 all-gather.8
  690.7 88.4 reduce-scatter.9
  829.5 66.1 all-gather.10
  910.7 88.5 reduce-scatter.11
  1065.2 149.8 all-reduce.9
  1218.7 63.0 reduce-scatter.13
  1285.6 56.6 all-reduce.11
  1347.9 129.0 all-reduce.7
where the time goes:
time: 1500 us; the launch traced here: 1490 us
  waiting for transfers between devices  806 us (54%)
  matrix products  291 us (19%)
  local copies, waits for them, and re-layouts  184 us (12%)
  other arithmetic  94.4 us (6%)
  blocking collectives  89.1 us (6%)
  between operations  17.4 us (1%)
    reduce_scatter x2, waiting for transfers between devices, body(): lax.psum_scatter(jnp.dot(activated, out_shard, preferred_element_type=jnp...  176 us
    reduce_scatter x2, waiting for transfers between devices, body(): lax.psum_scatter(jnp.dot(hidden_grad, in_shard, preferred_element_type=jn...  163 us
    all_gather x2, waiting for transfers between devices, body(): gathered = lax.all_gather(normed_low, 'tp', axis=0, tiled=True)  133 us
    all_gather x2, waiting for transfers between devices, body(): grad_rows = lax.all_gather(branch_grad, 'tp', axis=0, tiled=True)  132 us
    psum x1, waiting for transfers between devices, body(): lax.psum((jnp.stack(grad_bias_list), jnp.stack(grad_bout_list), jnp.stack...  128 us
    reduce_scatter x1, waiting for transfers between devices, body(): lax.psum_scatter(jnp.stack(grad_outw_list)[:, None].astype(jnp.bfloat16),...  64.6 us
    psum x1, blocking collectives, body(): lax.psum((part_gain, part_shift), ('seq', 'tp'))  42.5 us
    dot_general x2, matrix products, table_block(): jnp.einsum('lhqk,qkb->bh', block_item[8], hit_table, preferred_element_ty...  42.3 us
  transfers between devices with their start and end apart: 21, of which 12 were waited for; matrix products, arithmetic and copies ran while one was open for 26% of the time, Pallas kernels for 0%

commit v1 on v0

v1 whole, which is shorter than its diff:
```python
import jax
import jax.numpy as jnp
import numpy as np
from jax import lax
from jax.experimental import pallas as pl
from jax.experimental.pallas import tpu as pltpu
from jax.sharding import PartitionSpec as P

HEADS = 12
HEAD_DIM = 64
VIS_TOK = 49
VIS_SLOTS = 64
POS_BINS = 32
BOX_BINS = 64
LAYERS = 2
BUCKETS = POS_BINS + 2 * BOX_BINS

HALF_TEXT = 256
HALF_SLOTS = VIS_SLOTS // 2
ROWS = HALF_TEXT + HALF_SLOTS
KEYS = 640
PAIRS = HEADS // 2
LANES = 128
norm_epsilon = 1e-05
NEVER = -1e30
bf16 = jnp.bfloat16
f32 = jnp.float32
MIB = 1 << 20


def mesh_bits(axis):
    return (lax.axis_size(axis) - 1).bit_length()


def flipped(block, axis, bit):
    count = lax.axis_size(axis)
    return lax.ppermute(block, axis, [(i, i ^ (1 << bit)) for i in range(count)])


def total_over_all(value):
    for axis in ("tp", "seq"):
        for bit in range(mesh_bits(axis)):
            value = value + flipped(value, axis, bit)
    return value


def add_low(left, right):
    return (left.astype(f32) + right.astype(f32)).astype(bf16)


def scatter_sum(keep, send, order):
    bits = mesh_bits("tp")
    part = add_low(keep, flipped(send, "tp", 0))
    shape = part.shape[1:]
    part = part.reshape((2,) * (bits - 1) + shape)
    left = list(range(1, bits))
    for bit in order(bits):
        axis = len(left) - 1 - left.index(bit)
        low = lax.index_in_dim(part, 0, axis, keepdims=False)
        high = lax.index_in_dim(part, 1, axis, keepdims=False)
        part = add_low(low, flipped(high, "tp", bit))
        left.remove(bit)
    for bit in range(mesh_bits("seq")):
        part = add_low(part, flipped(part, "seq", bit))
    return part.astype(f32)


def low_first(bits):
    return list(range(1, bits))


def high_first(bits):
    return list(range(2, bits)) + [1]


def page_places(half, length, own_boxes, other_boxes):
    def slots(width, first, second):
        lane = lax.broadcasted_iota(jnp.int32, (1, width), 1)
        place = jnp.where(lane < HALF_SLOTS, first + lane, second + lane - HALF_SLOTS)
        place = jnp.where(lane < VIS_SLOTS, place, VIS_SLOTS - 1)
        row = (place * 37) >> 8
        return place, 71 + 143 * (place - 7 * row), 71 + 143 * row

    text = lax.broadcasted_iota(jnp.int32, (1, HALF_TEXT), 1)
    own_text = half * HALF_TEXT + text
    other_text = (1 - half) * HALF_TEXT + text
    slot = slots(LANES, half * HALF_SLOTS, (1 - half) * HALF_SLOTS)
    lane = lax.broadcasted_iota(jnp.int32, (1, LANES), 1)
    slot_used = jnp.where((slot[0] < VIS_TOK) & (lane < VIS_SLOTS), 1, 0)
    keys = (
        jnp.concatenate([own_text, other_text, slot[0]], axis=1),
        jnp.concatenate([own_boxes[0:1], other_boxes[0:1], slot[1]], axis=1),
        jnp.concatenate([own_boxes[1:2], other_boxes[1:2], slot[2]], axis=1),
        jnp.concatenate(
            [
                jnp.where(own_text < length, 1, 0),
                jnp.where(other_text < length, 1, 0),
                slot_used,
            ],
            axis=1,
        ),
    )
    queries = (
        jnp.concatenate([own_text, slot[0]], axis=1),
        jnp.concatenate([own_boxes[0:1], slot[1]], axis=1),
        jnp.concatenate([own_boxes[1:2], slot[2]], axis=1),
    )
    return keys, queries


def as_columns(rows):
    stacked = jnp.concatenate(list(rows) + [rows[0]] * (8 - len(rows)), axis=0)
    turned = jnp.transpose(stacked.astype(f32), (1, 0)).astype(jnp.int32)
    return [turned[:ROWS, i : i + 1] for i in range(len(rows))]


def bias_kernel(facts, own_boxes, other_boxes, table_a, table_b, out, near_s, across_s, down_s):
    @pl.when(pl.program_id(0) == 0)
    def _():
        keys, queries = page_places(facts[0], facts[1], own_boxes[...], other_boxes[...])
        place, x, y = as_columns(queries)
        near_s[...] = jnp.clip(keys[0] - place, -16, 15) + 16
        across_s[...] = jnp.clip((keys[1] - x) >> 4, -32, 31) + 64
        down_s[...] = jnp.where(
            keys[3] > 0, jnp.clip((keys[2] - y) >> 4, -32, 31) + 32, BOX_BINS
        )

    a = jnp.broadcast_to(table_a[0, 0:1, :], (ROWS, LANES))
    b = jnp.broadcast_to(table_b[0, 0:1, :], (ROWS, LANES))
    for tile in range(KEYS // LANES):
        span = slice(tile * LANES, (tile + 1) * LANES)

        def look(table, codes):
            return jnp.take_along_axis(table, codes, axis=1, mode="promise_in_bounds")

        out[0, :, span] = (
            look(a, near_s[:, span]) + look(a, across_s[:, span]) + look(b, down_s[:, span])
        )


def make_bias(facts, own_boxes, other_boxes, bias_table):
    columns = bias_table.T
    table_a = jnp.pad(columns[:, : POS_BINS + BOX_BINS], ((0, 0), (0, LANES - POS_BINS - BOX_BINS)))
    table_b = jnp.pad(
        columns[:, POS_BINS + BOX_BINS :],
        ((0, 0), (0, LANES - BOX_BINS)),
        constant_values=NEVER,
    )
    spread = lambda t: jnp.broadcast_to(t[:, None, :], (HEADS, 8, LANES))
    whole = lambda h, facts: (0, 0)
    return pl.pallas_call(
        bias_kernel,
        out_shape=jax.ShapeDtypeStruct((HEADS, ROWS, KEYS), f32),
        grid_spec=pltpu.PrefetchScalarGridSpec(
            num_scalar_prefetch=1,
            grid=(HEADS,),
            in_specs=[
                pl.BlockSpec((2, HALF_TEXT), whole),
                pl.BlockSpec((2, HALF_TEXT), whole),
                pl.BlockSpec((1, 8, LANES), lambda h, facts: (h, 0, 0)),
                pl.BlockSpec((1, 8, LANES), lambda h, facts: (h, 0, 0)),
            ],
            out_specs=pl.BlockSpec((1, ROWS, KEYS), lambda h, facts: (h, 0, 0)),
            scratch_shapes=[pltpu.VMEM((ROWS, KEYS), jnp.int32)] * 3,
        ),
        compiler_params=pltpu.CompilerParams(vmem_limit_bytes=24 * MIB),
        cost_estimate=pl.CostEstimate(
            flops=40 * HEADS * ROWS * KEYS,
            bytes_accessed=4 * HEADS * ROWS * KEYS,
            transcendentals=0,
        ),
        name="score_bias",
    )(facts, own_boxes, other_boxes, spread(table_a), spread(table_b))


def table_kernel(facts, own_boxes, other_boxes, ds_a, ds_b, out, right, left, band, cx, cy, high):
    @pl.when(pl.program_id(0) == 0)
    def _():
        keys, queries = page_places(facts[0], facts[1], own_boxes[...], other_boxes[...])
        place, x, y = as_columns(queries)
        diff = keys[0] - place
        band[...] = jnp.where((diff >= -16) & (diff <= 15), 1.0, 0.0).astype(bf16)
        high[...] = jnp.where(diff > 15, 1.0, 0.0).astype(bf16)
        cx[...] = jnp.where((keys[1] & 15) < (x & 15), 1.0, 0.0).astype(bf16)
        cy[...] = jnp.where((keys[2] & 15) < (y & 15), 1.0, 0.0).astype(bf16)
        row = lax.broadcasted_iota(jnp.int32, (64, KEYS), 0)
        key_hot = [
            jnp.where((63 - row) == (code & 63), 1.0, 0.0)
            for code in (keys[1] >> 4, keys[2] >> 4, keys[0])
        ]
        key_hot.append(jnp.zeros((64, KEYS), f32))
        right[...] = jnp.transpose(jnp.concatenate(key_hot, axis=0), (1, 0)).astype(bf16)
        row = lax.broadcasted_iota(jnp.int32, (64, 384), 0)
        query_hot = [
            jnp.where(row == queries[1] >> 4, 1.0, 0.0),
            jnp.where(row == queries[2] >> 4, 1.0, 0.0),
            jnp.where(row[:32] + 64 == queries[2] >> 4, 1.0, 0.0),
            jnp.where(row == (queries[0] & 63), 1.0, 0.0),
        ]
        left[...] = jnp.concatenate(query_hot, axis=0)[:, :ROWS].astype(bf16)

    total = (ds_a[0].astype(f32) + ds_b[0].astype(f32)).astype(bf16)
    hot = right[...]
    query_hot = left[...]

    def fold(values, columns, rows):
        inner = jnp.dot(values, hot[:, columns], preferred_element_type=f32).astype(bf16)
        return jnp.dot(query_hot[rows], inner, preferred_element_type=f32)

    plain = fold(total, slice(0, 128), slice(0, 160))
    by_x = fold(total * cx[...], slice(0, 128), slice(0, 64))
    by_y = fold(total * cy[...], slice(0, 128), slice(64, 160))
    near = fold(total * band[...], slice(128, 256), slice(160, 224))

    def diagonals(square):
        lane = lax.broadcasted_iota(jnp.int32, square.shape, 1)
        square = jnp.where(lane < 64, square, 0.0)
        turned = pltpu.roll(square, 0, axis=1, stride=1, stride_axis=0)
        return jnp.sum(turned, axis=0, keepdims=True)

    def second(square):
        return pltpu.roll(square, 64, axis=1)

    above = jnp.sum((total * high[...]).astype(f32), axis=0, keepdims=True)
    above = sum(above[:, t * LANES : (t + 1) * LANES] for t in range(KEYS // LANES))
    out[0] = jnp.concatenate(
        [
            diagonals(plain[:64]),
            diagonals(by_x),
            diagonals(second(plain[64:128])),
            diagonals(second(by_y[:64])),
            diagonals(near),
            above,
            diagonals(second(plain[128:])),
            diagonals(second(by_y[64:])),
        ],
        axis=0,
    )


def table_bins():
    bins = np.zeros((8, LANES, BUCKETS), np.float32)
    for c in range(127):
        diff = 63 - c
        for kind, base in ((0, POS_BINS), (1, POS_BINS + BOX_BINS)):
            here = base + 32 + min(max(diff, -32), 31)
            below = base + 32 + min(max(diff - 1, -32), 31)
            bins[2 * kind, c, here] += 1
            bins[2 * kind + 1, c, below] += 1
            bins[2 * kind + 1, c, here] -= 1
        far = -1 - c
        bins[6, c, 128 + max(far, -32)] += 1
        bins[7, c, 128 + max(far - 1, -32)] += 1
        bins[7, c, 128 + max(far, -32)] -= 1
        near = (diff + 32) % 64 - 32
        if -16 <= near <= 15:
            bins[4, c, near + 16] += 1
        bins[0, c, 0] += 1
        bins[4, c, 0] -= 1
    bins[5, :, 31] += 1
    bins[5, :, 0] -= 1
    return bins


def make_table_grad(facts, own_boxes, other_boxes, ds_a, ds_b):
    whole = lambda h, facts: (0, 0)
    head = pl.BlockSpec((1, ROWS, KEYS), lambda h, facts: (h, 0, 0))
    folded = pl.pallas_call(
        table_kernel,
        out_shape=jax.ShapeDtypeStruct((HEADS, 8, LANES), f32),
        grid_spec=pltpu.PrefetchScalarGridSpec(
            num_scalar_prefetch=1,
            grid=(HEADS,),
            in_specs=[
                pl.BlockSpec((2, HALF_TEXT), whole),
                pl.BlockSpec((2, HALF_TEXT), whole),
                head,
                head,
            ],
            out_specs=pl.BlockSpec((1, 8, LANES), lambda h, facts: (h, 0, 0)),
            scratch_shapes=[
                pltpu.VMEM((KEYS, 256), bf16),
                pltpu.VMEM((224, ROWS), bf16),
                pltpu.VMEM((ROWS, KEYS), bf16),
                pltpu.VMEM((ROWS, KEYS), bf16),
                pltpu.VMEM((ROWS, KEYS), bf16),
                pltpu.VMEM((ROWS, KEYS), bf16),
            ],
        ),
        compiler_params=pltpu.CompilerParams(vmem_limit_bytes=24 * MIB),
        cost_estimate=pl.CostEstimate(
            flops=HEADS * 2 * 4 * ROWS * KEYS * 256,
            bytes_accessed=4 * HEADS * ROWS * KEYS,
            transcendentals=0,
        ),
        name="table_grad",
    )(facts, own_boxes, other_boxes, ds_a, ds_b)
    bins = jnp.asarray(table_bins()).reshape(8 * LANES, BUCKETS)
    return lax.dot_general(
        bins,
        folded.reshape(HEADS, 8 * LANES),
        (((0,), (1,)), ((), ())),
        precision=lax.Precision.HIGHEST,
        preferred_element_type=f32,
    )


def whole_page(own, other):
    return jnp.concatenate(
        [
            own[:HALF_TEXT],
            other[:HALF_TEXT],
            own[HALF_TEXT:],
            other[HALF_TEXT:],
            jnp.zeros((KEYS - 2 * ROWS, own.shape[1]), own.dtype),
        ],
        axis=0,
    )


def page_split(both):
    mid = 2 * HALF_TEXT
    own = jnp.concatenate([both[:HALF_TEXT], both[mid : mid + HALF_SLOTS]], axis=0)
    other = jnp.concatenate(
        [both[HALF_TEXT:mid], both[mid + HALF_SLOTS : mid + VIS_SLOTS]], axis=0
    )
    return own, other


def nt_dot(left, right):
    return lax.dot_general(left, right, (((1,), (1,)), ((), ())), preferred_element_type=f32)


def tn_dot(left, right):
    return lax.dot_general(left, right, (((0,), (0,)), ((), ())), preferred_element_type=f32)


def attend_kernel(q_ref, ko, kp, vo, vp, bias, ctx, soft):
    q = q_ref[...] * jnp.asarray(HEAD_DIM**-0.5, bf16)
    keys = whole_page(ko[...], kp[...])
    values = whole_page(vo[...], vp[...])
    first = lax.broadcasted_iota(jnp.int32, (ROWS, LANES), 1) < HEAD_DIM
    parts = []
    for head in range(2):
        mine = jnp.where(first if head == 0 else ~first, q, jnp.zeros_like(q))
        scores = nt_dot(mine, keys) + bias[head]
        raised = jnp.exp(scores - jnp.max(scores, axis=1, keepdims=True))
        weights = (raised * (1.0 / jnp.sum(raised, axis=1, keepdims=True))).astype(bf16)
        soft[head] = weights
        parts.append(jnp.dot(weights, values, preferred_element_type=f32))
    ctx[...] = jnp.where(first, parts[0], parts[1]).astype(bf16)


def attend(q, ko, kp, vo, vp, bias):
    slab = pl.BlockSpec((ROWS, LANES), lambda p: (0, p))
    heads = pl.BlockSpec((2, ROWS, KEYS), lambda p: (p, 0, 0))
    return pl.pallas_call(
        attend_kernel,
        grid=(PAIRS,),
        in_specs=[slab] * 5 + [heads],
        out_specs=[slab, heads],
        out_shape=[
            jax.ShapeDtypeStruct(q.shape, bf16),
            jax.ShapeDtypeStruct((HEADS, ROWS, KEYS), bf16),
        ],
        compiler_params=pltpu.CompilerParams(vmem_limit_bytes=32 * MIB),
        cost_estimate=pl.CostEstimate(
            flops=HEADS * 4 * ROWS * KEYS * 256,
            bytes_accessed=6 * HEADS * ROWS * KEYS,
            transcendentals=HEADS * ROWS * KEYS,
        ),
        name="attend",
    )(q, ko, kp, vo, vp, bias)


def attend_back_kernel(q_ref, ko, kp, vo, vp, dc_ref, soft, dq, ds, dk_own, dk_other, dv_own, dv_other):
    scale = HEAD_DIM**-0.5
    q = q_ref[...]
    dc = dc_ref[...]
    keys = whole_page(ko[...], kp[...])
    values = whole_page(vo[...], vp[...])
    first = lax.broadcasted_iota(jnp.int32, (ROWS, LANES), 1) < HEAD_DIM
    q_turned = jnp.transpose(q.astype(f32), (1, 0)).astype(bf16)
    dc_turned = jnp.transpose(dc.astype(f32), (1, 0)).astype(bf16)
    dq_parts, dk_parts, dv_parts = [], [], []
    for head in range(2):
        span = slice(head * HEAD_DIM, (head + 1) * HEAD_DIM)
        mine = jnp.where(first if head == 0 else ~first, dc, jnp.zeros_like(dc))
        weights = soft[head]
        weights_f = weights.astype(f32)
        flow = nt_dot(mine, values)
        share = jnp.sum(weights_f * flow, axis=1, keepdims=True)
        score_grad = (weights_f * (flow - share)).astype(bf16)
        ds[head] = score_grad
        dq_parts.append(jnp.dot(score_grad, keys, preferred_element_type=f32))
        dk_parts.append(jnp.dot(q_turned[span], score_grad, preferred_element_type=f32))
        dv_parts.append(jnp.dot(dc_turned[span], weights, preferred_element_type=f32))
    dq[...] = (jnp.where(first, dq_parts[0], dq_parts[1]) * scale).astype(bf16)
    own, other = page_split(jnp.transpose(jnp.concatenate(dk_parts, axis=0) * scale, (1, 0)))
    dk_own[...] = own
    dk_other[...] = other.astype(bf16)
    own, other = page_split(jnp.transpose(jnp.concatenate(dv_parts, axis=0), (1, 0)))
    dv_own[...] = own
    dv_other[...] = other.astype(bf16)


def attend_back(q, ko, kp, vo, vp, dctx, soft):
    slab = pl.BlockSpec((ROWS, LANES), lambda p: (0, p))
    heads = pl.BlockSpec((2, ROWS, KEYS), lambda p: (p, 0, 0))
    low = jax.ShapeDtypeStruct(q.shape, bf16)
    wide = jax.ShapeDtypeStruct(q.shape, f32)
    return pl.pallas_call(
        attend_back_kernel,
        grid=(PAIRS,),
        in_specs=[slab] * 6 + [heads],
        out_specs=[slab, heads] + [slab] * 4,
        out_shape=[
            low,
            jax.ShapeDtypeStruct((HEADS, ROWS, KEYS), bf16),
            wide,
            low,
            wide,
            low,
        ],
        compiler_params=pltpu.CompilerParams(vmem_limit_bytes=32 * MIB),
        cost_estimate=pl.CostEstimate(
            flops=HEADS * 8 * ROWS * KEYS * 256,
            bytes_accessed=4 * HEADS * ROWS * KEYS,
            transcendentals=0,
        ),
        name="attend_back",
    )(q, ko, kp, vo, vp, dctx, soft)


def ffn_kernel(me, x_ref, own_w, mate_w, bias, act, slope, branch):
    step = pl.program_id(0)
    width = x_ref.shape[1]
    x = x_ref[...]

    @pl.when(step == 0)
    def _():
        branch[...] = jnp.zeros_like(branch)

    total = None
    for index, block in enumerate((own_w, mate_w)):
        weights = block[0]
        hidden = nt_dot(x, weights[:, :width]) + bias[pl.ds(me[0] ^ (2 * step + index), 1), :]
        half_cdf = 0.5 + 0.5 * lax.erf(hidden * 0.5**0.5)
        low = (hidden * half_cdf).astype(bf16)
        act[index] = low
        density = jnp.exp(hidden * hidden * -0.5) * (1.0 / (2.0 * np.pi) ** 0.5)
        slope[index] = (half_cdf + hidden * density).astype(bf16)
        term = jnp.dot(low, weights[:, width:], preferred_element_type=f32)
        total = term if total is None else total + term
    branch[...] += total


def ffn(me, layer, x, gathered, bias, units):
    groups = bias.shape[0]
    rows, width = x.shape
    whole = lambda i, me: (0, 0)
    pick = lambda which: pl.BlockSpec(
        (1, units, 2 * width), lambda i, me: (me[0] ^ (2 * i + which), layer, 0)
    )
    kept = pl.BlockSpec((2, rows, units), lambda i, me: (i, 0, 0))
    kept_shape = jax.ShapeDtypeStruct((groups, rows, units), bf16)
    return pl.pallas_call(
        ffn_kernel,
        out_shape=[kept_shape, kept_shape, jax.ShapeDtypeStruct((rows, width), f32)],
        grid_spec=pltpu.PrefetchScalarGridSpec(
            num_scalar_prefetch=1,
            grid=(groups // 2,),
            in_specs=[
                pl.BlockSpec((rows, width), whole),
                pick(0),
                pick(1),
                pl.BlockSpec(bias.shape, whole),
            ],
            out_specs=[kept, kept, pl.BlockSpec((rows, width), whole)],
        ),
        compiler_params=pltpu.CompilerParams(vmem_limit_bytes=32 * MIB),
        cost_estimate=pl.CostEstimate(
            flops=4 * rows * width * groups * units,
            bytes_accessed=4 * groups * units * (width + rows),
            transcendentals=2 * rows * groups * units,
        ),
        name="feed_forward",
    )(me, x, gathered, gathered, bias)


def ffn_back_kernel(me, x_ref, dy_ref, own_w, mate_w, act, slope, keep, send, bias_grad, dx):
    step = pl.program_id(0)
    width = x_ref.shape[1]
    x = x_ref[...]
    dy = dy_ref[...]

    @pl.when(step == 0)
    def _():
        dx[...] = jnp.zeros_like(dx)

    total = None
    for index, (block, out) in enumerate(((own_w, keep), (mate_w, send))):
        weights = block[0]
        flow = nt_dot(dy, weights[:, width:])
        grad = (flow * slope[index].astype(f32)).astype(bf16)
        bias_grad[index] = jnp.broadcast_to(
            jnp.sum(grad.astype(f32), axis=0, keepdims=True), bias_grad.shape[1:]
        )
        term = jnp.dot(grad, weights[:, :width], preferred_element_type=f32)
        total = term if total is None else total + term
        out[0, :, :width] = tn_dot(grad, x).astype(bf16)
        out[0, :, width:] = tn_dot(act[index], dy).astype(bf16)
    dx[...] += total


def ffn_back(me, layer, x, dy, gathered, act, slope):
    groups, rows, units = act.shape
    width = x.shape[1]
    whole = lambda i, me: (0, 0)
    pick = lambda which: pl.BlockSpec(
        (1, units, 2 * width), lambda i, me: (me[0] ^ (2 * i + which), layer, 0)
    )
    kept = pl.BlockSpec((2, rows, units), lambda i, me: (i, 0, 0))
    grads = pl.BlockSpec((1, units, 2 * width), lambda i, me: (i, 0, 0))
    grads_shape = jax.ShapeDtypeStruct((groups // 2, units, 2 * width), bf16)
    return pl.pallas_call(
        ffn_back_kernel,
        out_shape=[
            grads_shape,
            grads_shape,
            jax.ShapeDtypeStruct((groups, 8, units), f32),
            jax.ShapeDtypeStruct((rows, width), f32),
        ],
        grid_spec=pltpu.PrefetchScalarGridSpec(
            num_scalar_prefetch=1,
            grid=(groups // 2,),
            in_specs=[
                pl.BlockSpec((rows, width), whole),
                pl.BlockSpec((rows, width), whole),
                pick(0),
                pick(1),
                kept,
                kept,
            ],
            out_specs=[
                grads,
                grads,
                pl.BlockSpec((2, 8, units), lambda i, me: (i, 0, 0)),
                pl.BlockSpec((rows, width), whole),
            ],
        ),
        compiler_params=pltpu.CompilerParams(vmem_limit_bytes=32 * MIB),
        cost_estimate=pl.CostEstimate(
            flops=8 * rows * width * groups * units,
            bytes_accessed=4 * groups * units * (2 * width + rows),
            transcendentals=0,
        ),
        name="feed_forward_back",
    )(me, x, dy, gathered, gathered, act, slope)


def projection_kernel(me, x_ref, ctx_ref, dq, dk, dv, da, keep, send, whole_s):
    groups = 2 * keep.shape[0]
    rows = keep.shape[1]
    width = x_ref.shape[1]
    for index, (left, right) in enumerate(
        ((x_ref, dq), (x_ref, dk), (x_ref, dv), (ctx_ref, da))
    ):
        whole_s[...] = tn_dot(left[...], right[...])
        span = slice(index * width, (index + 1) * width)
        for place in range(groups):
            start = pl.multiple_of((me[0] ^ place) * rows, 8)
            target = keep if place % 2 == 0 else send
            target[place // 2, :, span] = whole_s[pl.ds(start, rows), :].astype(bf16)


def projection_grads(me, x, ctx, dq, dk, dv, da, groups):
    width = x.shape[1]
    vmem = pl.BlockSpec(memory_space=pltpu.VMEM)
    shape = jax.ShapeDtypeStruct((groups // 2, width // groups, 4 * width), bf16)
    return pl.pallas_call(
        projection_kernel,
        out_shape=[shape, shape],
        in_specs=[pl.BlockSpec(memory_space=pltpu.SMEM)] + [vmem] * 6,
        out_specs=[vmem, vmem],
        scratch_shapes=[pltpu.VMEM((width, width), f32)],
        compiler_params=pltpu.CompilerParams(vmem_limit_bytes=32 * MIB),
        cost_estimate=pl.CostEstimate(
            flops=8 * x.shape[0] * width * width,
            bytes_accessed=8 * width * width,
            transcendentals=0,
        ),
        name="projection_grads",
    )(me, x, ctx, dq, dk, dv, da)


def layer_norm(values, gain_row, shift_row):
    center = values - jnp.mean(values, axis=-1, keepdims=True)
    spread = jnp.mean(center * center, axis=-1, keepdims=True)
    return center * lax.rsqrt(spread + norm_epsilon) * gain_row + shift_row


def body(
    text_states,
    visual_maps,
    text_boxes,
    text_lengths,
    qkv_weight,
    out_weight,
    attn_bias,
    ffn_in,
    ffn_in_bias,
    ffn_out,
    ffn_out_bias,
    norm_gain,
    norm_shift,
    bias_table,
    vis_weight,
    vis_bias,
    bn_gain,
    bn_shift,
    cotangent,
):
    tp_index = lax.axis_index("tp")
    tp_size = lax.axis_size("tp")
    half = tp_index % 2
    page = (lax.axis_index("seq") * tp_size + tp_index) // 2
    me = tp_index.astype(jnp.int32).reshape(1)
    units = ffn_in.shape[1]
    width = text_states.shape[1]
    text_rows = text_states.shape[0]

    bias_rows = jnp.pad(ffn_in_bias, ((0, 16 - LAYERS), (0, 2 * width - units)))
    packed = jnp.concatenate(
        [
            jnp.concatenate([ffn_in, ffn_out], axis=2).reshape(LAYERS * units, 2 * width),
            bias_rows,
        ],
        axis=0,
    )
    gathered = lax.all_gather(packed, "tp", axis=0)
    hidden_bias = gathered[:, LAYERS * units : LAYERS * units + LAYERS, :units].astype(f32)

    other_boxes = flipped(text_boxes, "tp", 0)
    length = lax.dynamic_index_in_dim(text_lengths, page, 0, keepdims=False)
    facts = jnp.stack([half.astype(jnp.int32), length])
    score_bias = make_bias(facts, text_boxes, other_boxes, bias_table)

    count_cells = text_lengths.shape[0] * VIS_TOK
    maps_float = visual_maps.astype(f32)
    slot_place = half * HALF_SLOTS + jnp.arange(HALF_SLOTS, dtype=jnp.int32)
    slot_mask = (slot_place < VIS_TOK)[:, None]
    masked_maps = jnp.where(slot_mask, maps_float, 0.0)
    sums = total_over_all(
        jnp.stack([jnp.sum(masked_maps, axis=0), jnp.sum(masked_maps * masked_maps, axis=0)])
    )
    channel_mean = sums[0] / count_cells
    inverse_std = lax.rsqrt(sums[1] / count_cells - channel_mean * channel_mean + norm_epsilon)
    centered_hat = jnp.where(slot_mask, (maps_float - channel_mean) * inverse_std, 0.0)
    normal_low = jnp.where(slot_mask, centered_hat * bn_gain + bn_shift, 0.0).astype(bf16)
    visual_tokens = jnp.dot(normal_low, vis_weight, preferred_element_type=f32) + vis_bias
    states = jnp.concatenate([text_states.astype(f32), visual_tokens], axis=0)

    saved = []
    for layer in range(LAYERS):
        rounded = states.astype(bf16)
        project = lambda index: jnp.dot(
            rounded, qkv_weight[layer, index], preferred_element_type=f32
        )
        key_value = jnp.concatenate(
            [project(1).astype(bf16), (project(2) + attn_bias[layer, 1]).astype(bf16)], axis=1
        )
        other_key_value = flipped(key_value, "tp", 0)
        query = (project(0) + attn_bias[layer, 0]).astype(bf16)
        parts = (
            query,
            key_value[:, :width],
            other_key_value[:, :width],
            key_value[:, width:],
            other_key_value[:, width:],
        )
        context, soft = attend(*parts, score_bias)
        attended = (
            jnp.dot(context, out_weight[layer], preferred_element_type=f32) + attn_bias[layer, 2]
        )
        residual_one = states + attended
        normed = layer_norm(residual_one, norm_gain[layer, 0], norm_shift[layer, 0])
        normed_low = normed.astype(bf16)
        act, slope, branch = ffn(
            me, layer, normed_low, gathered, hidden_bias[:, layer], units
        )
        residual_two = normed + (branch + ffn_out_bias[layer])
        states = layer_norm(residual_two, norm_gain[layer, 1], norm_shift[layer, 1])
        saved.append((rounded, parts, soft, context, residual_one, normed_low, residual_two, act, slope))
    out_states = states.astype(bf16)

    gradient = cotangent.astype(f32)
    bias_grads = [None] * LAYERS
    bout_grads = [None] * LAYERS
    bin_grads = [None] * LAYERS
    gain_grads = [None] * LAYERS
    shift_grads = [None] * LAYERS
    ffn_shards = [None] * LAYERS
    projection_shards = [None] * LAYERS
    score_grads = [None] * LAYERS
    for layer in reversed(range(LAYERS)):
        rounded, parts, soft, context, residual_one, normed_low, residual_two, act, slope = saved[layer]
        grad_two, gain_two, shift_two = jax.vjp(
            layer_norm, residual_two, norm_gain[layer, 1], norm_shift[layer, 1]
        )[1](gradient)
        branch_grad = grad_two.astype(bf16)
        bout_grads[layer] = jnp.sum(branch_grad.astype(f32), axis=0)
        keep, send, bin_part, normed_grad = ffn_back(
            me, layer, normed_low, branch_grad, gathered, act, slope
        )
        bin_grads[layer] = bin_part[:, 0]
        ffn_shards[layer] = scatter_sum(keep, send, low_first)
        grad_one, gain_one, shift_one = jax.vjp(
            layer_norm, residual_one, norm_gain[layer, 0], norm_shift[layer, 0]
        )[1](grad_two + normed_grad)
        gain_grads[layer] = jnp.stack([gain_one, gain_two])
        shift_grads[layer] = jnp.stack([shift_one, shift_two])
        attended_grad = grad_one.astype(bf16)
        context_grad = nt_dot(attended_grad, out_weight[layer]).astype(bf16)
        query_grad, score_grads[layer], dk_own, dk_other, dv_own, dv_other = attend_back(
            *parts, context_grad, soft
        )
        back = flipped(jnp.concatenate([dk_other, dv_other], axis=1), "tp", 0)
        key_grad = (dk_own + back[:, :width].astype(f32)).astype(bf16)
        value_grad = (dv_own + back[:, width:].astype(f32)).astype(bf16)
        bias_grads[layer] = jnp.stack(
            [
                jnp.sum(query_grad.astype(f32), axis=0),
                jnp.sum(value_grad.astype(f32), axis=0),
                jnp.sum(attended_grad.astype(f32), axis=0),
            ]
        )
        gradient = grad_one + (
            nt_dot(query_grad, qkv_weight[layer, 0])
            + nt_dot(key_grad, qkv_weight[layer, 1])
            + nt_dot(value_grad, qkv_weight[layer, 2])
        )
        keep, send = projection_grads(
            me, rounded, context, query_grad, key_grad, value_grad, attended_grad, tp_size
        )
        projection_shards[layer] = scatter_sum(keep, send, high_first)

    table_grad = make_table_grad(facts, text_boxes, other_boxes, score_grads[0], score_grads[1])
    grad_text = gradient[:text_rows]
    token_grad = gradient[text_rows:].astype(bf16)
    vis_weight_grad = total_over_all(tn_dot(normal_low, token_grad).astype(bf16)).astype(f32)
    normal_grad = jnp.where(slot_mask, nt_dot(token_grad, vis_weight), 0.0)

    small = [
        jnp.stack(bias_grads).reshape(-1),
        jnp.stack(bout_grads).reshape(-1),
        jnp.stack(gain_grads).reshape(-1),
        jnp.stack(shift_grads).reshape(-1),
        table_grad.reshape(-1),
        jnp.sum(token_grad.astype(f32), axis=0),
        jnp.sum(normal_grad * centered_hat, axis=0),
        jnp.sum(normal_grad, axis=0),
        jnp.take(jnp.stack(bin_grads, axis=1), tp_index ^ jnp.arange(tp_size), axis=0).reshape(-1),
    ]
    sizes = [part.size for part in small]
    flat = jnp.concatenate(small)
    flat = jnp.pad(flat, (0, -flat.size % 1024)).reshape(-1, 128)
    flat = total_over_all(flat).reshape(-1)
    found = []
    start = 0
    for size in sizes:
        found.append(flat[start : start + size])
        start += size
    bias_total, bout_total, gain_total, shift_total, table_total, visb_total = found[:6]
    bn_gain_grad, bn_shift_grad, bin_total = found[6:]
    bin_total = lax.dynamic_index_in_dim(
        bin_total.reshape(tp_size, LAYERS, units), tp_index, 0, keepdims=False
    )
    grad_maps = jnp.where(
        slot_mask,
        inverse_std
        * (
            normal_grad * bn_gain
            - bn_gain * bn_shift_grad / count_cells
            - centered_hat * (bn_gain * bn_gain_grad / count_cells)
        ),
        0.0,
    )
    projections = jnp.stack(projection_shards).reshape(LAYERS, -1, 4, width)
    ffn_total = jnp.stack(ffn_shards)
    return (
        out_states,
        grad_text,
        grad_maps,
        projections[:, :, :3].transpose(0, 2, 1, 3),
        projections[:, :, 3],
        bias_total.reshape(attn_bias.shape),
        ffn_total[:, :, :width],
        bin_total,
        ffn_total[:, :, width:],
        bout_total.reshape(ffn_out_bias.shape),
        gain_total.reshape(norm_gain.shape),
        shift_total.reshape(norm_shift.shape),
        table_total.reshape(bias_table.shape),
        vis_weight_grad,
        visb_total,
        bn_gain_grad,
        bn_shift_grad,
    )


def solution(mesh):
    rows = P(("seq", "tp"), None)
    units = P(None, "tp", None)
    return jax.shard_map(
        body,
        mesh=mesh,
        in_specs=(
            rows,
            rows,
            P(None, ("seq", "tp")),
            P(),
            P(),
            P(),
            P(),
            units,
            P(None, "tp"),
            units,
            P(),
            P(),
            P(),
            P(),
            P(),
            P(),
            P(),
            P(),
            rows,
        ),
        out_specs=(
            rows,
            rows,
            rows,
            P(None, None, "tp", None),
            units,
            P(),
            units,
            P(None, "tp"),
            units,
            P(),
            P(),
            P(),
            P(),
            P(),
            P(),
            P(),
            P(),
        ),
        check_vma=False,
    )
```

time: 1500 us -> 650 us (0.43)
  waiting for transfers between devices: 806 us -> 286 us
  matrix products: 291 us -> 30.9 us
  Pallas kernels: 0 us -> 140 us
  local copies, waits for them, and re-layouts: 184 us -> 64.8 us
  blocking collectives: 89.1 us -> 0 us
  starting transfers between devices: 4.29 us -> 53 us
  other arithmetic: 94.4 us -> 54.3 us
    reduce_scatter x5 -> x0, waiting for transfers between devices: 403 us -> none  [the longest x2 176 us: body(): lax.psum_scatter(jnp.dot(activated, out_shard, preferred_element_type=jnp...]
    dot_general x45 -> x20, matrix products: 291 us -> 30.9 us  [the longest x9 14.4 us: nt_dot(): lax.dot_general(left, right, (((1,), (1,)), ((), ())), preferred_element_...]
    ppermute x9 -> x40, waiting for transfers between devices: 0.02 us -> 243 us  [flipped(): return lax.ppermute(block, axis, [(i, i ^ 1 << bit) for i in range(count)])]
    all_gather x4 -> x1, waiting for transfers between devices: 265 us -> 42.1 us  [body(): gathered = lax.all_gather(packed, 'tp', axis=0)]
    pallas_call x0 -> x12, Pallas kernels: none -> 140 us  [the longest x2 35.3 us: ffn_back(): pl.pallas_call(ffn_back_kernel, out_shape=[grads_shape, grads_shape, jax....]
    psum x2 -> x0, waiting for transfers between devices: 136 us -> none  [the longest x1 128 us: body(): lax.psum((jnp.stack(grad_bias_list), jnp.stack(grad_bout_list), jnp.stack...]
    psum x3 -> x0, blocking collectives: 89.1 us -> none  [the longest x1 42.5 us: body(): lax.psum((part_gain, part_shift), ('seq', 'tp'))]
    another operation x23 -> x10, local copies, waits for them, and re-layouts: 59 us -> 3.59 us  [the longest x2 2.35 us: body(): projections = jnp.stack(projection_shards).reshape(LAYERS, -1, 4, width)]
  transfers between devices with their start and end apart: 21 -> 41, of which waited for: 12 -> 25; matrix products, arithmetic and copies ran while one was open for 26% -> 12% of each run, Pallas kernels for 0% -> 9%
where the time goes in v1:
time: 650 us; the launch traced here: 645 us
  waiting for transfers between devices  286 us (44%)
  Pallas kernels  140 us (22%)
  local copies, waits for them, and re-layouts  64.8 us (10%)
  other arithmetic  54.3 us (8%)
  starting transfers between devices  53 us (8%)
  matrix products  30.9 us (5%)
  between operations  16.3 us (3%)
    ppermute x40, waiting for transfers between devices, flipped(): return lax.ppermute(block, axis, [(i, i ^ 1 << bit) for i in range(count)])  243 us
    ppermute x40, starting transfers between devices, flipped(): return lax.ppermute(block, axis, [(i, i ^ 1 << bit) for i in range(count)])  52.9 us
    unnamed x227, local copies, waits for them, and re-layouts  45.1 us
    all_gather x1, waiting for transfers between devices, body(): gathered = lax.all_gather(packed, 'tp', axis=0)  42.1 us
    pallas_call x2, Pallas kernels, ffn_back(): pl.pallas_call(ffn_back_kernel, out_shape=[grads_shape, grads_shape, jax....  35.3 us
    convert_element_type x18, other arithmetic, add_low(): return (left.astype(f32) + right.astype(f32)).astype(bf16)  24.5 us
    pallas_call x1, Pallas kernels, make_bias(): pl.pallas_call(bias_kernel, out_shape=jax.ShapeDtypeStruct((HEADS, ROWS,...  20.4 us
    pallas_call x2, Pallas kernels, ffn(): pl.pallas_call(ffn_kernel, out_shape=[kept_shape, kept_shape, jax.ShapeDt...  20 us
  transfers between devices with their start and end apart: 41, of which 25 were waited for; matrix products, arithmetic and copies ran while one was open for 12% of the time, Pallas kernels for 9%

profile of v1, /device:TPU:0, one launch (start us, length us, event | category | flops | bytes accessed | tf_op | source)
XLA Modules:
  0.0 644.7 jit_solution(11760249540775933211)
XLA Ops:
  11.4 2.9 collective-permute-start.1
  15.9 2.1 collective-permute-start.2
  19.6 3.0 collective-permute-start.3
  24.3 1.8 collective-permute-start.4
  28.2 2.1 convolution_convert_fusion.3.ko
  30.4 2.0 fusion.14.vo
  38.3 20.4 %score_bias.1.bias = f32[12,288,640]{2,1,0:T(8,128)S(1)} custom-call(s32[2]{0:T(128)S(1)} %pad_add_fusion.facts, s32[2,256]{1,0:T(2,128)S(1)} %copy-done.44, s32[2,256]{1,0:T(2,128)S(1)} %collective-permute-done.6.other_boxes, f32[12,8,128]{2,1,0:T(8,128)S(1)} %broadcast_in_dim.102.table_a, f32[12,8,128]{2,1,0:T(8,128)S(1)} %broadcast_in_dim.103.table_b), custom_call_target="tpu_custom_call" | custom-call | flops 88473600 | bytes 8847360 | tf_op jit(solution)/shard_map/score_bias/pallas_call | solution.py:151
  58.8 2.7 fusion.13.q_ref
  61.6 8.6 %attend.2 = (bf16[288,768]{1,0:T(8,128)(2,1)S(1)}, bf16[12,288,640]{2,1,0:T(8,128)(2,1)S(1)}) custom-call(bf16[288,768]{1,0:T(8,128)(2,1)S(1)} %fusion.13.q_ref, bf16[288,768]{1,0:T(8,128)(2,1)S(1)} %convolution_convert_fusion.3.ko, bf16[288,768]{1,0:T(8,128)(2,1)S(1)} %get-tuple-element.193.kp, bf16[288,768]{1,0:T(8,128)(2,1)S(1)} %fusion.14.vo, ...), custom_call_target="tpu_custom_call" | custom-call | flops 2264924160 | bytes 13271040 | tf_op jit(solution)/shard_map/attend/pallas_call | solution.py:357
  73.3 42.1 %all-gather.3.cloned.1.call-done = bf16[6400,1536]{1,0:T(8,128)(2,1)} async-done(((bf16[400,1536]{1,0:T(8,128)(2,1)}), bf16[6400,1536]{1,0:T(8,128)(2,1)}) %all-gather.3.cloned.1.call-update) | async-done | bytes 19660816 | tf_op jit(solution)/shard_map/all_gather | solution.py:641
  116.4 10.1 %feed_forward.2 = (bf16[16,288,192]{2,1,0:T(8,128)(2,1)S(1)}, bf16[16,288,192]{2,1,0:T(8,128)(2,1)S(1)}, f32[288,768]{1,0:T(8,128)S(1)}) custom-call(s32[1]{0:T(128)} %bitcast.10.me, bf16[288,768]{1,0:T(8,128)(2,1)S(1)} %fusion.62.x_ref, bf16[16,400,1536]{2,1,0:T(8,128)(2,1)} %bitcast.222, bf16[16,400,1536]{2,1,0:T(8,128)(2,1)} %bitcast.223, ...), custom_call_target="tpu_custom_call" | custom-call | flops 2717908992 | bytes 12976128 | tf_op jit(solution)/shard_map/feed_forward/pallas_call | solution.py:467
  127.8 1.9 convolution_convert_fusion.2.ko
  134.2 3.5 copy-done.2
  137.7 8.6 %attend.3 = (bf16[288,768]{1,0:T(8,128)(2,1)S(1)}, bf16[12,288,640]{2,1,0:T(8,128)(2,1)S(1)}) custom-call(bf16[288,768]{1,0:T(8,128)(2,1)S(1)} %fusion.15.q_ref, bf16[288,768]{1,0:T(8,128)(2,1)S(1)} %convolution_convert_fusion.2.ko, bf16[288,768]{1,0:T(8,128)(2,1)S(1)} %get-tuple-element.191.kp, bf16[288,768]{1,0:T(8,128)(2,1)S(1)} %fusion.16.vo, ...), custom_call_target="tpu_custom_call" | custom-call | flops 2264924160 | bytes 13271040 | tf_op jit(solution)/shard_map/attend/pallas_call | solution.py:357
  147.6 10.0 %feed_forward.3 = (bf16[16,288,192]{2,1,0:T(8,128)(2,1)S(1)}, bf16[16,288,192]{2,1,0:T(8,128)(2,1)S(1)}, f32[288,768]{1,0:T(8,128)S(1)}) custom-call(s32[1]{0:T(128)} %bitcast.10.me, bf16[288,768]{1,0:T(8,128)(2,1)S(1)} %fusion.64.x_ref, bf16[16,400,1536]{2,1,0:T(8,128)(2,1)} %bitcast.224, bf16[16,400,1536]{2,1,0:T(8,128)(2,1)} %bitcast.225, ...), custom_call_target="tpu_custom_call" | custom-call | flops 2717908992 | bytes 12976128 | tf_op jit(solution)/shard_map/feed_forward/pallas_call | solution.py:467
  160.3 17.8 %feed_forward_back.2 = (bf16[8,192,1536]{2,1,0:T(8,128)(2,1)S(1)}, bf16[8,192,1536]{2,1,0:T(8,128)(2,1)S(1)}, f32[16,8,192]{2,1,0:T(8,128)S(1)}, f32[288,768]{1,0:T(8,128)S(1)}) custom-call(s32[1]{0:T(128)} %bitcast.10.me, bf16[288,768]{1,0:T(8,128)(2,1)S(1)} %fusion.64.x_ref, bf16[288,768]{1,0:T(8,128)(2,1)S(1)} %get-tuple-element.158.dy_ref, ...), custom_call_target="tpu_custom_call" | custom-call | flops 5435817984 | bytes 22413312 | tf_op jit(solution)/shard_map/feed_forward_back/pallas_call | solution.py:526
  178.2 2.1 copy-done.45
  183.5 9.4 %attend_back.2 = (bf16[288,768]{1,0:T(8,128)(2,1)S(1)}, bf16[12,288,640]{2,1,0:T(8,128)(2,1)S(1)}, f32[288,768]{1,0:T(8,128)S(1)}, bf16[288,768]{1,0:T(8,128)(2,...) custom-call(bf16[288,768]{1,0:T(8,128)(2,1)S(1)} %fusion.15.q_ref, ...), custom_call_target="tpu_custom_call" | custom-call | flops 4529848320 | bytes 8847360 | tf_op jit(solution)/shard_map/attend_back/pallas_call | solution.py:412
  195.5 2.1 copy-done.53
  201.8 1.9 convert_reduce_fusion.4
  204.4 2.0 fusion.24
  208.2 2.1 multiply_reduce_fusion.1
  212.0 17.4 %feed_forward_back.3 = (bf16[8,192,1536]{2,1,0:T(8,128)(2,1)S(1)}, bf16[8,192,1536]{2,1,0:T(8,128)(2,1)S(1)}, f32[16,8,192]{2,1,0:T(8,128)S(1)}, f32[288,768]{1,0:T(8,128)S(1)}) custom-call(s32[1]{0:T(128)} %bitcast.10.me, bf16[288,768]{1,0:T(8,128)(2,1)S(1)} %fusion.62.x_ref, bf16[288,768]{1,0:T(8,128)(2,1)S(1)} %get-tuple-element.156.dy_ref, ...), custom_call_target="tpu_custom_call" | custom-call | flops 5435817984 | bytes 22413312 | tf_op jit(solution)/shard_map/feed_forward_back/pallas_call | solution.py:526
  229.4 2.1 copy-done.4
  231.6 2.2 copy-done.46
  238.7 2.0 convolution_convert_fusion.dc_ref
  240.8 2.2 copy-done.48
  243.0 9.4 %attend_back.3 = (bf16[288,768]{1,0:T(8,128)(2,1)S(1)}, bf16[12,288,640]{2,1,0:T(8,128)(2,1)S(1)}, f32[288,768]{1,0:T(8,128)S(1)}, bf16[288,768]{1,0:T(8,128)(2,...) custom-call(bf16[288,768]{1,0:T(8,128)(2,1)S(1)} %copy-done.43, bf16[288,768]{1,0:T(8,128)(2,1)S(1)} %copy-done.10, ...), custom_call_target="tpu_custom_call" | custom-call | flops 4529848320 | bytes 8847360 | tf_op jit(solution)/shard_map/attend_back/pallas_call | solution.py:412
  253.9 2.2 copy-done.54
  256.1 19.4 %table_grad.1 = f32[12,8,128]{2,1,0:T(8,128)S(1)} custom-call(s32[2]{0:T(128)S(1)} %pad_add_fusion.facts, s32[2,256]{1,0:T(2,128)S(1)} %copy-done.44, s32[2,256]{1,0:T(2,128)S(1)} %collective-permute-done.6.other_boxes, bf16[12,288,640]{2,1,0:T(8,128)(2,1)S(1)} %get-tuple-element.73.ds_a, bf16[12,288,640]{2,1,0:T(8,128)(2,1)S(1)} %copy-done.54), custom_call_target="tpu_custom_call" | custom-call | flops 4529848320 | bytes 8847360 | tf_op jit(solution)/shard_map/table_grad/pallas_call | solution.py:268
  282.4 4.4 projection_grads.3
  288.5 2.1 fusion.34
  292.6 1.9 fusion.12
  298.6 2.0 convolution_convert_fusion.4
  303.7 3.0 collective-permute-done.12
  306.7 2.4 collective-permute-start.13
  309.7 2.1 slice.369
  319.8 4.3 projection_grads.2
  328.7 9.6 %collective-permute-done.36 = bf16[256,768]{1,0:T(8,128)(2,1)S(1)} collective-permute-done((bf16[256,768]{1,0:T(8,128)(2,1)S(1)}, bf16[256,768]{1,0:T(8,128)(2,1)S(1)}, u32[]{:S(2)}, u32[]{:S(2)}) %collective-permute-start.36) | collective-permute-done | bytes 393248 | tf_op jit(solution)/shard_map/ppermute | solution.py:37
  345.3 4.1 collective-permute-done.37
  350.5 3.1 collective-permute-start.38
  353.7 2.5 add_convert_fusion.2
  356.2 14.3 %collective-permute-done.38 = bf16[256,768]{1,0:T(8,128)(2,1)S(1)} collective-permute-done((bf16[256,768]{1,0:T(8,128)(2,1)S(1)}, bf16[256,768]{1,0:T(8,128)(2,1)S(1)}, u32[]{:S(2)}, u32[]{:S(2)}) %collective-permute-start.38) | collective-permute-done | bytes 393248 | tf_op jit(solution)/shard_map/ppermute | solution.py:37
  372.1 8.7 %collective-permute-done.39 = bf16[256,768]{1,0:T(8,128)(2,1)S(1)} collective-permute-done((bf16[256,768]{1,0:T(8,128)(2,1)S(1)}, bf16[256,768]{1,0:T(8,128)(2,1)S(1)}, u32[]{:S(2)}, u32[]{:S(2)}) %collective-permute-start.39) | collective-permute-done | bytes 393248 | tf_op jit(solution)/shard_map/ppermute | solution.py:37
  381.7 3.1 add_convert_fusion.3
  387.5 12.7 %collective-permute-done.21 = bf16[2,2,48,3072]{3,2,1,0:T(8,128)(2,1)S(1)} collective-permute-done((bf16[2,2,48,3072]{3,2,1,0:T(8,128)(2,1)S(1)}, bf16[2,2,48,3072]{3,2,1,0:T(8,128)(2,1)S(1)}, u32[]{:S(2)}, u32[]{:S(2)}) %collective-permute-start.21) | collective-permute-done | bytes 1179680 | tf_op jit(solution)/shard_map/ppermute | solution.py:37
  400.7 2.0 collective-permute-start.22
  402.8 4.2 add_convert_fusion
  407.0 28.1 %collective-permute-done.22 = bf16[2,48,3072]{2,1,0:T(8,128)(2,1)S(1)} collective-permute-done((bf16[2,48,3072]{2,1,0:T(8,128)(2,1)S(1)}, bf16[2,48,3072]{2,1,0:T(8,128)(2,1)S(1)}, u32[]{:S(2)}, u32[]{:S(2)}) %collective-permute-start.22) | collective-permute-done | bytes 589856 | tf_op jit(solution)/shard_map/ppermute | solution.py:37
  439.3 5.9 collective-permute-done.23
  448.5 3.4 collective-permute-start.17
  452.0 4.0 add_convert_fusion.1
  456.0 17.5 %collective-permute-done.17 = bf16[2,48,3072]{2,1,0:T(8,128)(2,1)S(1)} collective-permute-done((bf16[2,48,3072]{2,1,0:T(8,128)(2,1)S(1)}, bf16[2,48,3072]{2,1,0:T(8,128)(2,1)S(1)}, u32[]{:S(2)}, u32[]{:S(2)}) %collective-permute-start.17) | collective-permute-done | bytes 589856 | tf_op jit(solution)/shard_map/ppermute | solution.py:37
  474.2 1.9 fusion.103
  479.2 23.0 %collective-permute-done.18 = bf16[48,3072]{1,0:T(8,128)(2,1)S(1)} collective-permute-done((bf16[48,3072]{1,0:T(8,128)(2,1)S(1)}, bf16[48,3072]{1,0:T(8,128)(2,1)S(1)}, u32[]{:S(2)}, u32[]{:S(2)}) %collective-permute-start.18) | collective-permute-done | bytes 294944 | tf_op jit(solution)/shard_map/ppermute | solution.py:37
  505.7 3.4 collective-permute-done.19
  512.1 2.4 fusion
  514.6 4.2 collective-permute-start.32
  518.8 31.8 %collective-permute-done.26 = bf16[2,2,192,1536]{3,2,0,1:T(8,128)(2,1)} collective-permute-done((bf16[2,2,192,1536]{3,2,0,1:T(8,128)(2,1)}, bf16[2,2,192,1536]{3,2,0,1:T(8,128)(2,1)}, u32[]{:S(2)}, u32[]{:S(2)}) %collective-permute-start.26) | collective-permute-done | bytes 2359328 | tf_op jit(solution)/shard_map/ppermute | solution.py:37
  550.6 2.4 fusion.1
  553.1 4.5 collective-permute-start.27
  558.4 36.2 %collective-permute-done.27 = bf16[2,192,1536]{2,1,0:T(8,128)(2,1)S(1)} collective-permute-done((bf16[2,192,1536]{2,1,0:T(8,128)(2,1)S(1)}, bf16[2,192,1536]{2,1,0:T(8,128)(2,1)S(1)}, u32[]{:S(2)}, u32[]{:S(2)}) %collective-permute-start.27) | collective-permute-done | bytes 1179680 | tf_op jit(solution)/shard_map/ppermute | solution.py:37
  596.8 23.5 %collective-permute-done.28 = bf16[192,1536]{1,0:T(8,128)(2,1)S(1)} collective-permute-done((bf16[192,1536]{1,0:T(8,128)(2,1)S(1)}, bf16[192,1536]{1,0:T(8,128)(2,1)S(1)}, u32[]{:S(2)}, u32[]{:S(2)}) %collective-permute-start.28) | collective-permute-done | bytes 589856 | tf_op jit(solution)/shard_map/ppermute | solution.py:37
  624.3 11.4 %collective-permute-done.29 = bf16[192,1536]{1,0:T(8,128)(2,1)S(1)} collective-permute-done((bf16[192,1536]{1,0:T(8,128)(2,1)S(1)}, bf16[192,1536]{1,0:T(8,128)(2,1)S(1)}, u32[]{:S(2)}, u32[]{:S(2)}) %collective-permute-start.29) | collective-permute-done | bytes 589856 | tf_op jit(solution)/shard_map/ppermute | solution.py:37
  (461 shorter events, 121.8 us)
Async XLA Ops:
  7.2 20.7 %copy-start = (bf16[256,768]{1,0:T(8,128)(2,1)S(1)}, bf16[256,768]{1,0:T(8,128)(2,1)}, u32[]{:S(2)}) copy-start(bf16[256,768]{1,0:T(8,128)(2,1)} %param.34) | copy-start | bytes 1179652
  7.2 108.2 %all-gather.3.cloned.1.call-start = ((), (), s32[]{:S(2)}) async-start(), calls=%async_computation | async-start | bytes 20889600 | tf_op jit(solution)/shard_map/all_gather | solution.py:641
  8.7 17.4 %copy-start.76 = (f32[2,3,768]{2,0,1:T(2,128)S(1)}, f32[2,3,768]{2,0,1:T(2,128)}, u32[]{:S(2)}) copy-start(f32[2,3,768]{2,0,1:T(2,128)} %param.26) | copy-start | bytes 55300
  8.7 18.1 %copy-start.69 = (bf16[256,768]{1,0:T(8,128)(2,1)S(1)}, bf16[256,768]{1,0:T(8,128)(2,1)}, u32[]{:S(2)}) copy-start(bf16[256,768]{1,0:T(8,128)(2,1)} %param.20) | copy-start | bytes 1179652
  8.7 19.2 %copy-start.77 = (f32[256]{0:T(256)S(1)}, f32[256]{0:T(256)}, u32[]{:S(2)}) copy-start(f32[256]{0:T(256)} %param.36) | copy-start | bytes 3076
  8.7 19.2 %copy-start.89 = (f32[768]{0:T(1024)S(1)}, f32[768]{0:T(1024)}, u32[]{:S(2)}) copy-start(f32[768]{0:T(1024)} %param.35) | copy-start | bytes 9220
  8.7 19.2 %copy-start.90 = (f32[256]{0:T(256)S(1)}, f32[256]{0:T(256)}, u32[]{:S(2)}) copy-start(f32[256]{0:T(256)} %param.37) | copy-start | bytes 3076
  9.9 20.4 %copy-start.83 = (pred[32]{0:T(512)(128)(4,1)}, pred[32]{0:T(512)(128)(4,1)S(1)}, u32[]{:S(2)}) copy-start(pred[32]{0:T(512)(128)(4,1)S(1)} %add_compare_fusion) | copy-start | bytes 100
  10.0 1.3 collective-permute-start
  11.4 4.5 collective-permute-start.1
  15.9 3.7 collective-permute-start.2
  19.6 4.7 collective-permute-start.3
  22.6 15.7 %collective-permute-start.6 = (s32[2,256]{1,0:T(2,128)S(1)}, s32[2,256]{1,0:T(2,128)S(1)}, u32[]{:S(2)}, u32[]{:S(2)}) collective-permute-start(s32[2,256]{1,0:T(2,128)S(1)} %copy-done.44), channel_id=1, source_target_pairs={{0,1},{1,0},{2,3},{3,2},{4,5},{5,4},{6,7},{7,6},{8,9},{9,8},{10,11... | collective-permute-start | bytes 6152 | tf_op jit(solution)/shard_map/ppermute | solution.py:37
  24.3 3.6 collective-permute-start.4
  28.2 30.5 %copy-start.34 = (bf16[288,768]{1,0:T(8,128)(2,1)}, bf16[288,768]{1,0:T(8,128)(2,1)S(1)}, u32[]{:S(2)}) copy-start(bf16[288,768]{1,0:T(8,128)(2,1)S(1)} %fusion.65.x_ref) | copy-start | bytes 1327108
  30.3 31.3 %copy-start.9 = (bf16[288,768]{1,0:T(8,128)(2,1)}, bf16[288,768]{1,0:T(8,128)(2,1)S(1)}, u32[]{:S(2)}) copy-start(bf16[288,768]{1,0:T(8,128)(2,1)S(1)} %convolution_convert_fusion.3.ko) | copy-start | bytes 1327108
  32.4 29.2 %copy-start.11 = (bf16[288,768]{1,0:T(8,128)(2,1)}, bf16[288,768]{1,0:T(8,128)(2,1)S(1)}, u32[]{:S(2)}) copy-start(bf16[288,768]{1,0:T(8,128)(2,1)S(1)} %fusion.14.vo) | copy-start | bytes 1327108
  33.4 28.1 %collective-permute-start.5 = (bf16[288,1536]{1,0:T(8,128)(2,1)}, bf16[288,1536]{1,0:T(8,128)(2,1)S(1)}, u32[]{:S(2)}, u32[]{:S(2)}) collective-permute-start(bf16[288,1536]{1,0:T(8,128)(2,1)} %pad_maximum_fusion.2), channel_id=1, source_target_pairs={{0,1},{1,0},{2,3},{3,2},{4,5},{5,4},{6,7},{7,6},{8,9},{9,8},{10,11... | collective-permute-start | bytes 2654216 | tf_op jit(solution)/shard_map/ppermute | solution.py:37
  36.1 36.4 %copy-start.70 = (f32[768]{0:T(1024)}, f32[768]{0:T(1024)S(1)}, u32[]{:S(2)}) copy-start(f32[768]{0:T(1024)S(1)} %get-tuple-element.147) | copy-start | bytes 9220
  38.3 20.5 %copy-start.96 = (f32[768]{0:T(1024)S(1)}, f32[768]{0:T(1024)}, u32[]{:S(2)}) copy-start(f32[768]{0:T(1024)} %get-tuple-element.137) | copy-start | bytes 9220
  126.9 19.5 %copy-start.59 = (f32[288,768]{1,0:T(8,128)}, f32[288,768]{1,0:T(8,128)S(1)}, u32[]{:S(2)}) copy-start(f32[288,768]{1,0:T(8,128)S(1)} %get-tuple-element.180) | copy-start | bytes 2654212
  131.7 2.5 collective-permute-start.7
  198.7 3.2 collective-permute-start.8
  212.0 21.8 %copy-start.57 = (f32[288,768]{1,0:T(8,128)S(1)}, f32[288,768]{1,0:T(8,128)}, u32[]{:S(2)}) copy-start(f32[288,768]{1,0:T(8,128)} %copy-done.55) | copy-start | bytes 2654212
  252.4 23.1 %copy-start.30 = (f32[288,768]{1,0:T(8,128)}, f32[288,768]{1,0:T(8,128)S(1)}, u32[]{:S(2)}) copy-start(f32[288,768]{1,0:T(8,128)S(1)} %get-tuple-element.69) | copy-start | bytes 2654212
  252.4 23.1 %copy-start.32 = (f32[288,768]{1,0:T(8,128)}, f32[288,768]{1,0:T(8,128)S(1)}, u32[]{:S(2)}) copy-start(f32[288,768]{1,0:T(8,128)S(1)} %get-tuple-element.72) | copy-start | bytes 2654212
  253.5 33.6 %collective-permute-start.9 = (bf16[288,1536]{1,0:T(8,128)(2,1)}, bf16[288,1536]{1,0:T(8,128)(2,1)}, u32[]{:S(2)}, u32[]{:S(2)}) collective-permute-start(bf16[288,1536]{1,0:T(8,128)(2,1)} %pad_maximum_fusion.5), channel_id=1, source_target_pairs={{0,1},{1,0},{2,3},{3,2},{4,5},{5,4},{6,7},{7,6},{8,9},{9,8},{10,11... | collective-permute-start | bytes 2654216 | tf_op jit(solution)/shard_map/ppermute | solution.py:37
  256.1 19.5 %copy-start.67 = (f32[8,128,160]{1,2,0:T(8,128)S(1)}, f32[8,128,160]{1,2,0:T(8,128)}, u32[]{:S(2)}) copy-start(f32[8,128,160]{1,2,0:T(8,128)} %constant.102.clone) | copy-start | bytes 1966084
  286.8 66.8 %collective-permute-start.20 = (bf16[8,48,3072]{2,1,0:T(8,128)(2,1)}, bf16[8,48,3072]{2,1,0:T(8,128)(2,1)}, u32[]{:S(2)}, u32[]{:S(2)}) collective-permute-start(bf16[8,48,3072]{2,1,0:T(8,128)(2,1)} %get-tuple-element.80), channel_id=1, source_target_pairs={{0,1},{1,0},{2,3},{3,2},{4,5},{5,4},{6,7},{7,6},{8,9},{9,8},{10,11... | collective-permute-start | bytes 7077896 | tf_op jit(solution)/shard_map/ppermute | solution.py:37
  295.9 1.4 collective-permute-start.10
  297.2 4.9 collective-permute-start.11
  300.6 25.0 %collective-permute-start.35 = (bf16[256,768]{1,0:T(8,128)(2,1)}, bf16[256,768]{1,0:T(8,128)(2,1)}, u32[]{:S(2)}, u32[]{:S(2)}) collective-permute-start(bf16[256,768]{1,0:T(8,128)(2,1)} %convolution_convert_fusion.4), channel_id=1, source_target_pairs={{0,1},{1,0},{2,3},{3,2},{4,5},{5,4},{6,7},{7,6},{8,9},{9,8},{10,11... | collective-permute-start | bytes 1179656 | tf_op jit(solution)/shard_map/ppermute | solution.py:37
  302.1 4.6 collective-permute-start.12
  306.7 5.6 collective-permute-start.13
  309.2 93.6 %collective-permute-start.30 = (bf16[8,192,1536]{2,1,0:T(8,128)(2,1)}, bf16[8,192,1536]{2,1,0:T(8,128)(2,1)}, u32[]{:S(2)}, u32[]{:S(2)}) collective-permute-start(bf16[8,192,1536]{2,1,0:T(8,128)(2,1)} %copy-done.45), channel_id=1, source_target_pairs={{0,1},{1,0},{2,3},{3,2},{4,5},{5,4},{6,7},{7,6},{8,9},{9,8},{10,11... | collective-permute-start | bytes 14155784 | tf_op jit(solution)/shard_map/ppermute | solution.py:37
  309.2 142.8 %collective-permute-start.25 = (bf16[8,192,1536]{2,1,0:T(8,128)(2,1)}, bf16[8,192,1536]{2,1,0:T(8,128)(2,1)}, u32[]{:S(2)}, u32[]{:S(2)}) collective-permute-start(bf16[8,192,1536]{2,1,0:T(8,128)(2,1)} %copy-done.46), channel_id=1, source_target_pairs={{0,1},{1,0},{2,3},{3,2},{4,5},{5,4},{6,7},{7,6},{8,9},{9,8},{10,11... | collective-permute-start | bytes 14155784 | tf_op jit(solution)/shard_map/ppermute | solution.py:37
  313.2 13.5 %collective-permute-start.14 = (f32[176,128]{1,0:T(8,128)S(1)}, f32[176,128]{1,0:T(8,128)S(1)}, u32[]{:S(2)}, u32[]{:S(2)}) collective-permute-start(f32[176,128]{1,0:T(8,128)S(1)} %add.464), channel_id=1, source_target_pairs={{0,16},{16,0},{1,17},{17,1},{2,18},{18,2},{3,19},{19,3},{4,20},{20... | collective-permute-start | bytes 270344 | tf_op jit(solution)/shard_map/ppermute | solution.py:37
  325.6 56.2 %collective-permute-start.15 = (bf16[8,48,3072]{2,1,0:T(8,128)(2,1)}, bf16[8,48,3072]{2,1,0:T(8,128)(2,1)}, u32[]{:S(2)}, u32[]{:S(2)}) collective-permute-start(bf16[8,48,3072]{2,1,0:T(8,128)(2,1)} %get-tuple-element.78), channel_id=1, source_target_pairs={{0,1},{1,0},{2,3},{3,2},{4,5},{5,4},{6,7},{7,6},{8,9},{9,8},{10,11... | collective-permute-start | bytes 7077896 | tf_op jit(solution)/shard_map/ppermute | solution.py:37
  326.8 11.6 %collective-permute-start.36 = (bf16[256,768]{1,0:T(8,128)(2,1)S(1)}, bf16[256,768]{1,0:T(8,128)(2,1)S(1)}, u32[]{:S(2)}, u32[]{:S(2)}) collective-permute-start(bf16[256,768]{1,0:T(8,128)(2,1)S(1)} %add.487), channel_id=1, source_target_pairs={{0,2},{1,3},{2,0},{3,1},{4,6},{5,7},{6,4},{7,5},{8,10},{9,11},{10,... | collective-permute-start | bytes 1179656 | tf_op jit(solution)/shard_map/ppermute | solution.py:37
  338.5 10.9 %collective-permute-start.37 = (bf16[256,768]{1,0:T(8,128)(2,1)S(1)}, bf16[256,768]{1,0:T(8,128)(2,1)}, u32[]{:S(2)}, u32[]{:S(2)}) collective-permute-start(bf16[256,768]{1,0:T(8,128)(2,1)S(1)} %add.488), channel_id=1, source_target_pairs={{0,4},{1,5},{2,6},{3,7},{4,0},{5,1},{6,2},{7,3},{8,12},{9,13},{10,... | collective-permute-start | bytes 1179656 | tf_op jit(solution)/shard_map/ppermute | solution.py:37
  350.5 20.0 %collective-permute-start.38 = (bf16[256,768]{1,0:T(8,128)(2,1)S(1)}, bf16[256,768]{1,0:T(8,128)(2,1)S(1)}, u32[]{:S(2)}, u32[]{:S(2)}) collective-permute-start(bf16[256,768]{1,0:T(8,128)(2,1)S(1)} %add.489), channel_id=1, source_target_pairs={{0,8},{1,9},{2,10},{3,11},{4,12},{5,13},{6,14},{7,15},{8,0},{9,1},... | collective-permute-start | bytes 1179656 | tf_op jit(solution)/shard_map/ppermute | solution.py:37
  356.2 25.5 %copy-start.8 = (bf16[8,48,3072]{2,1,0:T(8,128)(2,1)S(1)}, bf16[8,48,3072]{2,1,0:T(8,128)(2,1)}, u32[]{:S(2)}) copy-start(bf16[8,48,3072]{2,1,0:T(8,128)(2,1)} %copy-done.7) | copy-start | bytes 7077892
  370.6 10.2 %collective-permute-start.39 = (bf16[256,768]{1,0:T(8,128)(2,1)S(1)}, bf16[256,768]{1,0:T(8,128)(2,1)S(1)}, u32[]{:S(2)}, u32[]{:S(2)}) collective-permute-start(bf16[256,768]{1,0:T(8,128)(2,1)S(1)} %add.490), channel_id=1, source_target_pairs={{0,16},{16,0},{1,17},{17,1},{2,18},{18,2},{3,19},{19,3},{4,20},{20... | collective-permute-start | bytes 1179656 | tf_op jit(solution)/shard_map/ppermute | solution.py:37
  371.3 29.0 %collective-permute-start.21 = (bf16[2,2,48,3072]{3,2,1,0:T(8,128)(2,1)S(1)}, bf16[2,2,48,3072]{3,2,1,0:T(8,128)(2,1)S(1)}, u32[]{:S(2)}, u32[]{:S(2)}) collective-permute-start(bf16[2,2,48,3072]{3,2,1,0:T(8,128)(2,1)S(1)} %slice_bitcast_fusion.5), channel_id=1, source_target_pairs={{0,4},{1,5},{2,6},{3,7},{4,0},{5,1},{6,2},{7,3},{8,12},{9,13},{10,... | collective-permute-start | bytes 3538952 | tf_op jit(solution)/shard_map/ppermute | solution.py:37
  380.8 22.0 %slice-start = ((s8[4718592]{0:T(1024)(128)(4,1)}), s8[4194304]{0:T(1024)(128)(4,1)S(1)}, s32[]{:S(2)}) async-start(s8[4718592]{0:T(1024)(128)(4,1)} %bitcast.217), calls=%async_computation.1 | async-start | bytes 8388608
  381.7 21.1 %slice-start.1 = ((s8[4718592]{0:T(1024)(128)(4,1)}), s8[524288]{0:T(1024)(128)(4,1)S(1)}, s32[]{:S(2)}) async-start(s8[4718592]{0:T(1024)(128)(4,1)} %bitcast.217), calls=%async_computation.2 | async-start | bytes 1048576
  386.0 60.9 %collective-permute-start.16 = (bf16[2,2,48,3072]{3,2,1,0:T(8,128)(2,1)}, bf16[2,2,48,3072]{3,2,1,0:T(8,128)(2,1)}, u32[]{:S(2)}, u32[]{:S(2)}) collective-permute-start(bf16[2,2,48,3072]{3,2,1,0:T(8,128)(2,1)} %slice_bitcast_fusion.7), channel_id=1, source_target_pairs={{0,4},{1,5},{2,6},{3,7},{4,0},{5,1},{6,2},{7,3},{8,12},{9,13},{10,... | collective-permute-start | bytes 3538952 | tf_op jit(solution)/shard_map/ppermute | solution.py:37
  400.7 34.3 %collective-permute-start.22 = (bf16[2,48,3072]{2,1,0:T(8,128)(2,1)S(1)}, bf16[2,48,3072]{2,1,0:T(8,128)(2,1)S(1)}, u32[]{:S(2)}, u32[]{:S(2)}) collective-permute-start(bf16[2,48,3072]{2,1,0:T(8,128)(2,1)S(1)} %slice_bitcast_fusion.13), channel_id=1, source_target_pairs={{0,8},{1,9},{2,10},{3,11},{4,12},{5,13},{6,14},{7,15},{8,0},{9,1},... | collective-permute-start | bytes 1769480 | tf_op jit(solution)/shard_map/ppermute | solution.py:37
  435.2 10.0 %collective-permute-start.23 = (bf16[48,3072]{1,0:T(8,128)(2,1)S(1)}, bf16[48,3072]{1,0:T(8,128)(2,1)S(1)}, u32[]{:S(2)}, u32[]{:S(2)}) collective-permute-start(bf16[48,3072]{1,0:T(8,128)(2,1)S(1)} %slice_bitcast_fusion.17), channel_id=1, source_target_pairs={{0,2},{1,3},{2,0},{3,1},{4,6},{5,7},{6,4},{7,5},{8,10},{9,11},{10,... | collective-permute-start | bytes 884744 | tf_op jit(solution)/shard_map/ppermute | solution.py:37
  435.8 16.2 %slice-start.2 = ((s8[4718592]{0:T(1024)(128)(4,1)}), s8[4194304]{0:T(1024)(128)(4,1)S(1)}, s32[]{:S(2)}) async-start(s8[4718592]{0:T(1024)(128)(4,1)} %bitcast.219), calls=%async_computation.3 | async-start | bytes 8388608
  436.2 15.7 %slice-start.3 = ((s8[4718592]{0:T(1024)(128)(4,1)}), s8[524288]{0:T(1024)(128)(4,1)S(1)}, s32[]{:S(2)}) async-start(s8[4718592]{0:T(1024)(128)(4,1)} %bitcast.219), calls=%async_computation.4 | async-start | bytes 1048576
  437.8 74.3 %collective-permute-start.31 = (bf16[2,2,192,1536]{3,2,0,1:T(8,128)(2,1)}, bf16[2,2,192,1536]{3,2,0,1:T(8,128)(2,1)}, u32[]{:S(2)}, u32[]{:S(2)}) collective-permute-start(bf16[2,2,192,1536]{3,2,0,1:T(8,128)(2,1)} %bitcast.214), channel_id=1, source_target_pairs={{0,2},{1,3},{2,0},{3,1},{4,6},{5,7},{6,4},{7,5},{8,10},{9,11},{10,... | collective-permute-start | bytes 7077896 | tf_op jit(solution)/shard_map/ppermute | solution.py:37
  445.3 58.4 %collective-permute-start.24 = (bf16[48,3072]{1,0:T(8,128)(2,1)S(1)}, bf16[48,3072]{1,0:T(8,128)(2,1)S(1)}, u32[]{:S(2)}, u32[]{:S(2)}) collective-permute-start(bf16[48,3072]{1,0:T(8,128)(2,1)S(1)} %fusion.68), channel_id=1, source_target_pairs={{0,16},{16,0},{1,17},{17,1},{2,18},{18,2},{3,19},{19,3},{4,20},{20... | collective-permute-start | bytes 884744 | tf_op jit(solution)/shard_map/ppermute | solution.py:37
  448.5 24.9 %collective-permute-start.17 = (bf16[2,48,3072]{2,1,0:T(8,128)(2,1)S(1)}, bf16[2,48,3072]{2,1,0:T(8,128)(2,1)S(1)}, u32[]{:S(2)}, u32[]{:S(2)}) collective-permute-start(bf16[2,48,3072]{2,1,0:T(8,128)(2,1)S(1)} %slice_bitcast_fusion.15), channel_id=1, source_target_pairs={{0,8},{1,9},{2,10},{3,11},{4,12},{5,13},{6,14},{7,15},{8,0},{9,1},... | collective-permute-start | bytes 1769480 | tf_op jit(solution)/shard_map/ppermute | solution.py:37
  473.6 28.5 %collective-permute-start.18 = (bf16[48,3072]{1,0:T(8,128)(2,1)S(1)}, bf16[48,3072]{1,0:T(8,128)(2,1)S(1)}, u32[]{:S(2)}, u32[]{:S(2)}) collective-permute-start(bf16[48,3072]{1,0:T(8,128)(2,1)S(1)} %slice_bitcast_fusion.19), channel_id=1, source_target_pairs={{0,2},{1,3},{2,0},{3,1},{4,6},{5,7},{6,4},{7,5},{8,10},{9,11},{10,... | collective-permute-start | bytes 884744 | tf_op jit(solution)/shard_map/ppermute | solution.py:37
  477.7 72.9 %collective-permute-start.26 = (bf16[2,2,192,1536]{3,2,0,1:T(8,128)(2,1)}, bf16[2,2,192,1536]{3,2,0,1:T(8,128)(2,1)}, u32[]{:S(2)}, u32[]{:S(2)}) collective-permute-start(bf16[2,2,192,1536]{3,2,0,1:T(8,128)(2,1)} %bitcast.215), channel_id=1, source_target_pairs={{0,2},{1,3},{2,0},{3,1},{4,6},{5,7},{6,4},{7,5},{8,10},{9,11},{10,... | collective-permute-start | bytes 7077896 | tf_op jit(solution)/shard_map/ppermute | solution.py:37
  502.2 6.9 %collective-permute-start.19 = (bf16[48,3072]{1,0:T(8,128)(2,1)S(1)}, bf16[48,3072]{1,0:T(8,128)(2,1)}, u32[]{:S(2)}, u32[]{:S(2)}) collective-permute-start(bf16[48,3072]{1,0:T(8,128)(2,1)S(1)} %fusion.69), channel_id=1, source_target_pairs={{0,16},{16,0},{1,17},{17,1},{2,18},{18,2},{3,19},{19,3},{4,20},{20... | collective-permute-start | bytes 884744 | tf_op jit(solution)/shard_map/ppermute | solution.py:37
  514.5 36.1 %copy-start.61 = (bf16[2,2,1,192,1536]{4,3,2,1,0:T(8,128)(2,1)S(1)}, bf16[2,2,1,192,1536]{4,3,2,1,0:T(8,128)(2,1)}, u32[]{:S(2)}) copy-start(bf16[2,2,1,192,1536]{4,3,2,1,0:T(8,128)(2,1)} %get-tuple-element.181) | copy-start | bytes 7077892
  514.6 43.4 %collective-permute-start.32 = (bf16[2,192,1536]{2,1,0:T(8,128)(2,1)S(1)}, bf16[2,192,1536]{2,1,0:T(8,128)(2,1)S(1)}, u32[]{:S(2)}, u32[]{:S(2)}) collective-permute-start(bf16[2,192,1536]{2,1,0:T(8,128)(2,1)S(1)} %slice_bitcast_fusion), channel_id=1, source_target_pairs={{0,4},{1,5},{2,6},{3,7},{4,0},{5,1},{6,2},{7,3},{8,12},{9,13},{10,... | collective-permute-start | bytes 3538952 | tf_op jit(solution)/shard_map/ppermute | solution.py:37
  553.1 41.5 %collective-permute-start.27 = (bf16[2,192,1536]{2,1,0:T(8,128)(2,1)S(1)}, bf16[2,192,1536]{2,1,0:T(8,128)(2,1)S(1)}, u32[]{:S(2)}, u32[]{:S(2)}) collective-permute-start(bf16[2,192,1536]{2,1,0:T(8,128)(2,1)S(1)} %slice_bitcast_fusion.2), channel_id=1, source_target_pairs={{0,4},{1,5},{2,6},{3,7},{4,0},{5,1},{6,2},{7,3},{8,12},{9,13},{10,... | collective-permute-start | bytes 3538952 | tf_op jit(solution)/shard_map/ppermute | solution.py:37
  558.3 36.7 %collective-permute-start.33 = (bf16[192,1536]{1,0:T(8,128)(2,1)S(1)}, bf16[192,1536]{1,0:T(8,128)(2,1)S(1)}, u32[]{:S(2)}, u32[]{:S(2)}) collective-permute-start(bf16[192,1536]{1,0:T(8,128)(2,1)S(1)} %slice_bitcast_fusion.9), channel_id=1, source_target_pairs={{0,8},{1,9},{2,10},{3,11},{4,12},{5,13},{6,14},{7,15},{8,0},{9,1},... | collective-permute-start | bytes 1769480 | tf_op jit(solution)/shard_map/ppermute | solution.py:37
  594.9 25.4 %collective-permute-start.28 = (bf16[192,1536]{1,0:T(8,128)(2,1)S(1)}, bf16[192,1536]{1,0:T(8,128)(2,1)S(1)}, u32[]{:S(2)}, u32[]{:S(2)}) collective-permute-start(bf16[192,1536]{1,0:T(8,128)(2,1)S(1)} %slice_bitcast_fusion.11), channel_id=1, source_target_pairs={{0,8},{1,9},{2,10},{3,11},{4,12},{5,13},{6,14},{7,15},{8,0},{9,1},... | collective-permute-start | bytes 1769480 | tf_op jit(solution)/shard_map/ppermute | solution.py:37
  595.2 28.9 %collective-permute-start.34 = (bf16[192,1536]{1,0:T(8,128)(2,1)S(1)}, bf16[192,1536]{1,0:T(8,128)(2,1)S(1)}, u32[]{:S(2)}, u32[]{:S(2)}) collective-permute-start(bf16[192,1536]{1,0:T(8,128)(2,1)S(1)} %fusion.18), channel_id=1, source_target_pairs={{0,16},{16,0},{1,17},{17,1},{2,18},{18,2},{3,19},{19,3},{4,20},{20... | collective-permute-start | bytes 1769480 | tf_op jit(solution)/shard_map/ppermute | solution.py:37
  620.4 15.3 %collective-permute-start.29 = (bf16[192,1536]{1,0:T(8,128)(2,1)S(1)}, bf16[192,1536]{1,0:T(8,128)(2,1)S(1)}, u32[]{:S(2)}, u32[]{:S(2)}) collective-permute-start(bf16[192,1536]{1,0:T(8,128)(2,1)S(1)} %fusion.19), channel_id=1, source_target_pairs={{0,16},{16,0},{1,17},{17,1},{2,18},{18,2},{3,19},{19,3},{4,20},{20... | collective-permute-start | bytes 1769480 | tf_op jit(solution)/shard_map/ppermute | solution.py:37
  (83 other events, 307.4 us)
Sparse Core Ops, SparseCore 0:
  10.0 105.3 all-gather.2
